TPU v7x, 256 devices: a whole 4x4x8 slice. The times are simulated.
256 devices in a mesh: beam: 4 (over z_lo, core), det: 16 (over y, x), slab: 4 (over z_hi).
Axes of the slice: x: 4, y: 4, z: 8 (z_hi: 4, z_lo: 2; z = z_hi * 2 + z_lo), core: 2. Of those that a mesh axis runs over, the one named last changes fastest.
Arguments:
- concentration: float32 [4, 32, 1024, 2048], P(None, 'slab', 'beam', 'det'), may hold values from 0.1 to 1
- cross_section: float32 [4, 16], replicated, may hold values from 0.2 to 2
- line_attenuation: float32 [4], replicated, may hold values from 0.5 to 2
- energy_index: int32 [4], replicated, may hold values from 0 to 15
- fan_offset: int32 [256], replicated, may hold values from 0 to 28
- fan_weight: int32 [256, 4], replicated, may hold values from 1 to 3
- measured: float32 [4, 256, 2048], P(None, None, 'det'), may hold values from 0 to 6
Outputs:
- voxel_grad: float32 [4, 32, 1024, 2048], P(None, 'slab', 'beam', 'det')
- residual: float32 [4, 256, 2048], P(None, ('beam', 'slab'), 'det')
All inputs are finite; a program needn't handle non-finite values.
Results may differ from a plain program's by a relative error of at most 0.00013.
Values sent between devices are 32-bit elements; how exact they have to be, the bound alone decides.
A program may use at most 128 MiB of HBM per device.

v0:
```python
import jax
import jax.numpy as jnp
from jax import lax
from jax.sharding import PartitionSpec as P


def entering(value, axis, join, neutral, backward):
    count, mine = (lax.axis_size(axis), lax.axis_index(axis))
    pieces = lax.all_gather(value, axis)
    if backward:
        pieces = pieces[::-1]
        mine = count - 1 - mine
    running = jnp.full_like(value, 0) + jnp.asarray(neutral, value.dtype)

    def lap(position, running):
        longer = join(running, pieces[position])
        return jnp.where(position < mine, longer, running)

    return lax.fori_loop(0, count - 1, lap, running)


def add_pair(earlier, later):
    return earlier + later


def fan_matrix(fan_offset, fan_weight, slices):
    taps = fan_offset[:, None] + jnp.arange(fan_weight.shape[1], dtype=jnp.int32)[None, :]
    match = (taps[:, :, None] == slices[None, None, :]).astype(jnp.float32)
    return jnp.sum(fan_weight.astype(jnp.float32)[:, :, None] * match, axis=1)


def shards(
    concentration, cross_section, line_attenuation, energy_index, fan_offset, fan_weight, measured
):
    highest = lax.Precision.HIGHEST
    n_species = concentration.shape[0]
    depth_z = concentration.shape[1]
    rows_x = concentration.shape[2]
    n_beam = lax.axis_size("beam")
    n_det = lax.axis_size("det")
    n_slab = lax.axis_size("slab")
    full_x = rows_x * n_beam
    full_y = concentration.shape[3] * n_det
    onehot = (
        energy_index[:, None] == jnp.arange(cross_section.shape[1], dtype=jnp.int32)[None, :]
    ).astype(jnp.float32)
    sigma_sel = jnp.sum(cross_section[:, None, :] * onehot[None], axis=2)
    n_energy = sigma_sel.shape[1]
    emission = sigma_sel[0][:, None, None, None] * concentration[0][None]
    absorber = line_attenuation[0] * concentration[0]
    for species in range(1, n_species):
        emission = emission + sigma_sel[species][:, None, None, None] * concentration[species][None]
        absorber = absorber + line_attenuation[species] * concentration[species]
    local_depth = jnp.sum(emission, axis=2)
    upstream = entering(local_depth, "beam", add_pair, jnp.zeros_like(local_depth), False)
    path_in = jnp.cumsum(emission, axis=2) - emission + upstream[:, :, None, :]
    incident = jnp.exp(-(1.5 / full_x) * path_in)
    row_depth = jnp.sum(absorber, axis=2)
    downstream = entering(row_depth, "det", add_pair, jnp.zeros_like(row_depth), True)
    path_out = row_depth[:, :, None] - jnp.cumsum(absorber, axis=2) + downstream[:, :, None]
    escape = jnp.exp(-(1.5 / full_y) * path_out)
    fluor = emission * incident * escape[None]
    line_sums = jnp.sum(fluor, axis=2)
    slab_index = lax.axis_index("slab")
    local_slices = slab_index * depth_z + jnp.arange(depth_z, dtype=jnp.int32)
    weights_local = fan_matrix(fan_offset, fan_weight, local_slices)
    group_index = lax.axis_index(("beam", "slab"))
    share = fan_offset.shape[0] // (n_beam * n_slab)
    first_row = group_index * share
    partial_signal = jnp.einsum("kz,ezy->eky", weights_local, line_sums, precision=highest) / full_x
    signal = lax.psum(partial_signal, ("beam", "slab"))
    misfit = signal - measured
    back = jnp.einsum("kz,eky->ezy", weights_local, misfit, precision=highest)
    residual = lax.dynamic_slice_in_dim(misfit, first_row, share, 1)
    heavy = back[:, :, None, :] * fluor
    heavy_rows = jnp.sum(heavy, axis=2)
    further = entering(heavy_rows, "beam", add_pair, jnp.zeros_like(heavy_rows), True)
    after_x = heavy_rows[:, :, None, :] - jnp.cumsum(heavy, axis=2) + further[:, :, None, :]
    heavy_all = jnp.sum(heavy, axis=0)
    column_sums = jnp.sum(heavy_all, axis=2)
    nearer = entering(column_sums, "det", add_pair, jnp.zeros_like(column_sums), False)
    before_y = jnp.cumsum(heavy_all, axis=2) - heavy_all + nearer[:, :, None]
    term = back[:, :, None, :] * incident * escape[None] - 1.5 / full_x * after_x
    result = []
    for species in range(n_species):
        accum = sigma_sel[species, 0] * term[0]
        for energy in range(1, n_energy):
            accum = accum + sigma_sel[species, energy] * term[energy]
        result.append(accum - line_attenuation[species] * (1.5 / full_y) * before_y)
    return (jnp.stack(result), residual)


def solution(mesh):
    in_specs = (P(None, "slab", "beam", "det"), P(), P(), P(), P(), P(), P(None, None, "det"))
    out_specs = (P(None, "slab", "beam", "det"), P(None, ("beam", "slab"), "det"))
    return jax.shard_map(shards, mesh=mesh, in_specs=in_specs, out_specs=out_specs, check_vma=False)
```

profile of v0, /device:TPU:1, one launch (start us, length us, event | category | flops | bytes accessed | tf_op | source)
XLA Modules:
  0.0 311.9 jit_solution(3524492392284493037)
XLA Ops:
  8.7 7.9 %slice_bitcast_fusion.11 = (f32[8,256,128]{2,1,0:T(8,128)S(1)}, f32[8,256,128]{2,1,0:T(8,128)S(1)}, f32[8,256,128]{2,1,0:T(8,128)}, f32[8,256,128]{2,1,0:T(8,128...) fusion(f32[4,8,256,128]{3,2,1,0:T(8,128)} %param.15, ...), kind=kLoop, calls=%fused_computation.80 | loop fusion | flops 1835008 | bytes 13631504 | tf_op jit(solution)/shard_map/mul | solution.py:49
  16.6 3.4 %add_reduce_fusion = f32[8,256]{1,0:T(8,128)} fusion(f32[]{:T(128)} %bitcast.24, f32[]{:T(128)} %bitcast.23, f32[]{:T(128)} %bitcast.22, f32[]{:T(128)} %bitcast.21, f32[4,8,256,128]{3,2,1,0:T(8,128)S(1)} %copy-done), kind=kLoop, calls=%fused_computation.58 | loop fusion | flops 2095104 | bytes 4202512 | tf_op jit(solution)/shard_map/reduce_sum | solution.py:58
  27.8 2.4 broadcast_add_fusion.1
  30.2 5.6 %copy.84 = f32[4,8,128,256]{3,1,2,0:T(8,128)} copy(f32[4,8,128,256]{2,1,3,0:T(8,128)} %bitcast.120) | data formatting | bytes 8388608 | tf_op jit(solution)/shard_map/reduce_window_sum
  38.4 3.0 copy.79
  41.4 2.5 fusion.12
  44.0 8.3 %all-gather = f32[16,8,128]{2,1,0:T(8,128)S(1)} all-gather(f32[4,8,128]{2,1,0:T(8,128)S(1)} %copy.85), channel_id=2, replica_groups=mesh['beam'=4,'det'=16,'slab'=4] {'beam'}, dimensions={0}, use_global_device_ids=true | all-gather | bytes 81920 | tf_op jit(solution)/shard_map/all_gather | solution.py:9
  52.5 2.7 copy.87
  55.2 17.2 %all-gather.1 = f32[128,256]{1,0:T(8,128)S(1)} all-gather(f32[8,256]{1,0:T(8,128)} %add_reduce_fusion), channel_id=3, replica_groups=mesh['beam'=4,'det'=16,'slab'=4] {'det'}, dimensions={0}, use_global_device_ids=true | all-gather | bytes 139264 | tf_op jit(solution)/shard_map/all_gather | solution.py:9
  72.4 18.8 %while.57 = (s32[]{:T(128)}, f32[8,256]{1,0:T(8,128)}, s32[]{:T(128)}, f32[16,8,256]{2,1,0:T(8,128)S(1)}, s32[]{:T(128)}, /*index=5*/s32[]{:T(128)}) while((s32[]{:T(128)}, f32[8,256]{1,0:T(8,128)}, s32[]{:T(128)}, f32[16,8,256]{2,1,0:T(8,128)S(1)}, s32[]{:T(128)}, /*index=5*/s32[]{:T(128)}) %tuple.155), condition=%wide.region_9.10_spmd.clone, body=%wide.region_8.9_spmd.clone.sunk | while | flops 6148 | bytes 24669 | solution.py:19
  94.1 6.2 %fusion.40 = (f32[4,8,128]{1,2,0:T(8,128)S(1)}, f32[4,8,256,128]{2,1,3,0:T(8,128)}) fusion(f32[8,256,128]{1,0,2:T(8,128)S(1)} %multiply_exponential_fusion, f32[4,8,128]{1,2,0:T(8,128)S(1)} %copy.86, f32[4,8,128,256]{3,1,2,0:T(8,128)} %copy.84, f32[8,256,128]{1,0,2:T(8,128)} %copy.79, f32[4]{0:T(128)} %copy-done.16, f32[8,256,128]{1,0,2:T(8,128)} %copy-done.1, ...), kind=kLoop, calls=%fused_computation.81 | loop fusion | flops 13627392 | bytes 13664320 | tf_op jit(solution)/shard_map/reduce_sum | solution.py:63
  108.6 108.6 %all-reduce.2.cloned.1.call-done = f32[4,256,128]{1,2,0:T(8,128)} async-done(((f32[4,256,128]{1,2,0:T(8,128)}), f32[4,256,128]{1,2,0:T(8,128)}) %all-reduce.2.cloned.1.call-update) | async-done | bytes 524304 | tf_op jit(solution)/shard_map/psum | solution.py:71
  220.0 4.1 %multiply_reduce_fusion.2 = (f32[4,8,128]{1,2,0:T(8,128)}, f32[8,256,128]{1,0,2:T(8,128)}, f32[8,256]{1,0:T(8,128)S(1)}) fusion(f32[4,8,256,128]{2,1,3,0:T(8,128)} %get-tuple-element.428, f32[4,8,128]{1,2,0:T(8,128)S(1)} %copy.91), kind=kLoop, calls=%fused_computation.25 | loop fusion | flops 3926016 | bytes 5283840 | tf_op jit(solution)/shard_map/reduce_sum | solution.py:76
  225.2 6.2 %all-gather.2 = f32[16,8,128]{2,1,0:T(8,128)} all-gather(f32[4,8,128]{2,1,0:T(8,128)S(1)} %copy.94), channel_id=4, replica_groups=mesh['beam'=4,'det'=16,'slab'=4] {'beam'}, dimensions={0}, use_global_device_ids=true | all-gather | bytes 81920 | tf_op jit(solution)/shard_map/all_gather | solution.py:9
  233.2 4.9 %fusion.3 = f32[4,8,128,2,128]{2,1,4,3,0:T(8,128)S(1)} fusion(f32[4,8,128,2,128]{2,1,4,3,0:T(8,128)} %broadcast_add_fusion.1, f32[8,128,2,128]{1,0,3,2:T(8,128)} %copy.92, f32[4,8,128]{2,1,0:T(8,128)S(1)} %get-tuple-element.318, f32[4,8,128]{2,1,0:T(8,128)S(1)} %convolution_bitcast_fusion, f32[8,128,2,128]{1,0,3,2:T(8,128)} %copy-done.5, ...), kind=kOutput, calls=%fused_computation.10 | output fusion | flops 146800640 | bytes 13664320 | tf_op jit(solution)/shard_map/reduce-window.2
  238.3 2.4 broadcast_add_fusion
  240.6 5.5 %copy.93 = f32[4,8,128,256]{3,1,2,0:T(8,128)} copy(f32[4,8,128,256]{2,1,3,0:T(8,128)} %bitcast.121) | data formatting | bytes 8388608 | tf_op jit(solution)/shard_map/reduce_window_sum
  248.5 20.0 %all-gather.3 = f32[128,256]{1,0:T(8,128)} all-gather(f32[8,256]{1,0:T(8,128)S(1)} %get-tuple-element.392), channel_id=5, replica_groups=mesh['beam'=4,'det'=16,'slab'=4] {'det'}, dimensions={0}, use_global_device_ids=true | all-gather | bytes 139264 | tf_op jit(solution)/shard_map/all_gather | solution.py:9
  268.5 10.5 %while.59 = (s32[]{:T(128)}, f32[8,256]{1,0:T(8,128)S(1)}, s32[]{:T(128)}, f32[16,8,256]{2,1,0:T(8,128)}, s32[]{:T(128)}, /*index=5*/s32[]{:T(128)}) while((s32[]{:T(128)}, f32[8,256]{1,0:T(8,128)S(1)}, s32[]{:T(128)}, f32[16,8,256]{2,1,0:T(8,128)}, s32[]{:T(128)}, /*index=5*/s32[]{:T(128)}) %tuple.170), condition=%wide.region_22.23_spmd.clone, body=%wide.region_21.22_spmd.clone.sunk | while | flops 6148 | bytes 24669 | solution.py:19
  279.0 6.3 %bitcast_subtract_fusion = f32[4,8,256,128]{2,1,3,0:T(8,128)S(1)} fusion(f32[4,8,128,256]{3,1,2,0:T(8,128)} %copy.93, f32[4,8,128]{1,2,0:T(8,128)} %copy.95, f32[4,8,128]{1,2,0:T(8,128)} %get-tuple-element.390, f32[4,8,128]{1,2,0:T(8,128)S(1)} %copy.91, f32[8,256,128]{1,0,2:T(8,128)S(1)} %multiply_exponential_fusion, f32[4,8,128]{1,2,0:T(8,128)} %copy-done.11, ...), kind=kLoop, calls=%fused_computation.5 | loop fusion | flops 16777216 | bytes 17891392 | tf_op jit(solution)/shard_map/sub | solution.py:83
  285.3 2.9 multiply_subtract_fusion.3
  288.3 2.9 multiply_subtract_fusion
  291.2 5.4 %multiply_subtract_fusion.2 = (f32[1,8,256,128]{2,1,3,0:T(8,128)S(1)}, f32[1,8,256,128]{2,1,3,0:T(8,128)S(1)}) fusion(f32[1,8,256,128]{2,1,3,0:T(8,128)S(1)} %get-tuple-element.426, f32[4,8,256,128]{2,1,3,0:T(8,128)S(1)} %bitcast_subtract_fusion, f32[]{:T(128)S(6)} %mul.559, f32[]{:T(128)} %bitcast.44, f32[]{:T(128)} %bitcast.43, f32[]{:T(128)} %bitcast.42, ...), kind=kLoop, calls=%fused_computation.54 | loop fusion | flops 4718592 | bytes 7340072 | tf_op jit(solution)/shard_map/sub | solution.py:89
  298.8 5.3 %copy.96 = f32[4,8,256,128]{3,2,1,0:T(8,128)} copy(f32[4,8,256,128]{2,1,3,0:T(8,128)} %pad_maximum_fusion) | data formatting | bytes 8388608
  (130 shorter events, 61.3 us)
Async XLA Ops:
  7.2 210.0 %all-reduce.2.cloned.1.call-start = ((), (), s32[]{:S(2)}) async-start(), calls=%async_computation | async-start | bytes 1048576 | tf_op jit(solution)/shard_map/psum | solution.py:71
  8.7 7.9 %copy-start = (f32[4,8,256,128]{3,2,1,0:T(8,128)S(1)}, f32[4,8,256,128]{3,2,1,0:T(8,128)}, u32[]{:S(2)}) copy-start(f32[4,8,256,128]{3,2,1,0:T(8,128)} %param.15) | copy-start | bytes 12582916
  20.0 4.2 %copy-start.7 = (f32[1,8,256,128]{3,2,1,0:T(8,128)S(1)}, f32[1,8,256,128]{3,2,1,0:T(8,128)}, u32[]{:S(2)}) copy-start(f32[1,8,256,128]{3,2,1,0:T(8,128)} %get-tuple-element.439) | copy-start | bytes 3145732
  20.0 5.4 %copy-start.23 = (s32[4]{0:T(128)S(1)}, s32[4]{0:T(128)}, u32[]{:S(2)}) copy-start(s32[4]{0:T(128)} %param.18) | copy-start | bytes 52
  20.0 5.5 %copy-start.22 = (f32[4,16]{1,0:T(4,128)S(1)}, f32[4,16]{1,0:T(4,128)}, u32[]{:S(2)}) copy-start(f32[4,16]{1,0:T(4,128)} %param.16) | copy-start | bytes 772
  21.9 5.6 %copy-start.2 = (f32[8,128,2,128]{1,0,3,2:T(8,128)}, f32[8,128,2,128]{1,0,3,2:T(8,128)S(1)}, u32[]{:S(2)}) copy-start(f32[8,128,2,128]{1,0,3,2:T(8,128)S(1)} %copy.80) | copy-start | bytes 3145732
  24.2 3.4 %copy-start.3 = (f32[8,128,2,128]{1,0,3,2:T(8,128)}, f32[8,128,2,128]{1,0,3,2:T(8,128)S(1)}, u32[]{:S(2)}) copy-start(f32[8,128,2,128]{1,0,3,2:T(8,128)S(1)} %copy.81) | copy-start | bytes 3145732
  24.8 2.8 copy-start.4
  25.4 2.1 copy-start.5
  25.6 15.8 %copy-start.14 = (f32[4]{0:T(128)}, f32[4]{0:T(128)S(1)}, u32[]{:S(2)}) copy-start(f32[4]{0:T(128)S(1)} %get-tuple-element.456) | copy-start | bytes 52
  25.6 15.8 %copy-start.16 = (f32[4]{0:T(128)}, f32[4]{0:T(128)S(1)}, u32[]{:S(2)}) copy-start(f32[4]{0:T(128)S(1)} %get-tuple-element.457) | copy-start | bytes 52
  25.6 15.8 %copy-start.18 = (f32[4]{0:T(128)}, f32[4]{0:T(128)S(1)}, u32[]{:S(2)}) copy-start(f32[4]{0:T(128)S(1)} %get-tuple-element.458) | copy-start | bytes 52
  25.7 15.7 %copy-start.20 = (f32[4]{0:T(128)}, f32[4]{0:T(128)S(1)}, u32[]{:S(2)}) copy-start(f32[4]{0:T(128)S(1)} %get-tuple-element.459) | copy-start | bytes 52
  38.4 16.9 %copy-start.1 = (f32[8,256,128]{1,0,2:T(8,128)}, f32[8,256,128]{1,0,2:T(8,128)S(1)}, u32[]{:S(2)}) copy-start(f32[8,256,128]{1,0,2:T(8,128)S(1)} %copy.78) | copy-start | bytes 3145732
  52.5 47.9 %copy-start.11 = (f32[4,8,128]{1,2,0:T(8,128)}, f32[4,8,128]{1,2,0:T(8,128)S(1)}, u32[]{:S(2)}) copy-start(f32[4,8,128]{1,2,0:T(8,128)S(1)} %copy.86) | copy-start | bytes 49156
  100.4 7.6 %copy-start.13 = (f32[4,4]{1,0:T(4,128)S(1)}, f32[4,4]{1,0:T(4,128)}, u32[]{:S(2)}) copy-start(f32[4,4]{1,0:T(4,128)} %copy-done.12) | copy-start | bytes 196
  218.5 0.8 copy-start.9
  219.3 13.9 %copy-start.15 = (f32[4]{0:T(128)S(1)}, f32[4]{0:T(128)}, u32[]{:S(2)}) copy-start(f32[4]{0:T(128)} %copy-done.14) | copy-start | bytes 52
  219.3 13.9 %copy-start.17 = (f32[4]{0:T(128)S(1)}, f32[4]{0:T(128)}, u32[]{:S(2)}) copy-start(f32[4]{0:T(128)} %copy-done.16) | copy-start | bytes 52
  219.3 13.9 %copy-start.19 = (f32[4]{0:T(128)S(1)}, f32[4]{0:T(128)}, u32[]{:S(2)}) copy-start(f32[4]{0:T(128)} %copy-done.18) | copy-start | bytes 52
  219.3 13.9 %copy-start.21 = (f32[4]{0:T(128)S(1)}, f32[4]{0:T(128)}, u32[]{:S(2)}) copy-start(f32[4]{0:T(128)} %copy-done.20) | copy-start | bytes 52
  279.0 6.3 %copy-start.6 = (f32[8,256,128]{1,0,2:T(8,128)S(1)}, f32[8,256,128]{1,0,2:T(8,128)}, u32[]{:S(2)}) copy-start(f32[8,256,128]{1,0,2:T(8,128)} %get-tuple-element.391) | copy-start | bytes 3145732
  279.0 6.3 %copy-start.8 = (f32[8,256,128]{1,0,2:T(8,128)S(1)}, f32[8,256,128]{1,0,2:T(8,128)}, u32[]{:S(2)}) copy-start(f32[8,256,128]{1,0,2:T(8,128)} %fusion.43) | copy-start | bytes 3145732
  298.8 5.4 %copy-start.10 = (f32[4,256,128]{1,2,0:T(8,128)S(1)}, f32[4,256,128]{1,2,0:T(8,128)}, u32[]{:S(2)}) copy-start(f32[4,256,128]{1,2,0:T(8,128)} %copy-done.9) | copy-start | bytes 1572868
  (1 other events, 0.8 us)
Sparse Core Ops, SparseCore 0:
  102.0 115.1 all-reduce.1
where the time goes:
time: 318 us; the launch traced here: 312 us
  waiting for transfers between devices  109 us (34%)
  other arithmetic  91.1 us (29%)
  blocking collectives  51.7 us (16%)
  local copies, waits for them, and re-layouts  41.4 us (13%)
  between operations  16.9 us (5%)
    psum x1, waiting for transfers between devices, shards(): signal = lax.psum(partial_signal, ('beam', 'slab'))  109 us
    all_gather x4, blocking collectives, entering(): pieces = lax.all_gather(value, axis)  51.7 us
    select_n x36, other arithmetic, lap(): return jnp.where(position < mine, longer, running)  29.4 us
    sub x3, other arithmetic, shards(): result.append(accum - line_attenuation[species] * (1.5 / full_y) * before_y)  11.3 us
    another operation x6, other arithmetic  11.1 us
    another operation x4, local copies, waits for them, and re-layouts  11.1 us
    unnamed x51, local copies, waits for them, and re-layouts  9.73 us
    mul x6, local copies, waits for them, and re-layouts, shards(): sigma_sel[species][:, None, None, None] * concentration[species][None]  8.59 us
  transfers between devices with their start and end apart: 1, of which 1 were waited for; matrix products, arithmetic and copies ran while one was open for 1% of the time, Pallas kernels for 0%

commit v1 on v0

v1 whole, which is shorter than its diff:
```python
import functools

import jax
import jax.numpy as jnp
from jax import lax
from jax.experimental import pallas as pl
from jax.experimental.pallas import tpu as pltpu
from jax.sharding import PartitionSpec as P

MESH = pl.DeviceIdType.MESH
F32 = jnp.float32
BF16 = jnp.bfloat16
HIGHEST = lax.Precision.HIGHEST
CHUNKS = 4
BLOCK = 16
REACH = 3


def split_pair(value):
    high = value.astype(BF16)
    low = (value - high.astype(F32)).astype(BF16)
    return jnp.concatenate([high, low], axis=1)


def row_totals(pair):
    ones = jnp.ones((8, pair.shape[1]), BF16)
    total = lax.dot_general(ones, pair, (((1,), (1,)), ((), ())), preferred_element_type=F32)
    return total[0:1]


def spread(compact):
    rows = compact.shape[0]
    padded = jnp.concatenate([compact, jnp.zeros((128 - rows, 128), F32)], axis=0)
    turned = jnp.transpose(padded)
    return [jnp.broadcast_to(turned[:, r : r + 1], (128, 128)) for r in range(rows)]


def kernel(
    sizes, conc, cross, lam, index, offset, weight, measured, out, resid,
    c_buf, em, inc, dmp, hl, meas, wt, wx, wk, band, wm, up_buf,
    ra_send, ra_recv, ud_send, ud_recv, x_buf, xl, la, rc_send, rc_recv,
    in_sem, meas_sem, ra_ss, ra_rs, ud_ss, ud_rs, x_ss, x_rs, la_ss, la_rs, rc_ss, rc_rs, out_sem,
):
    n_beam, n_det, n_slab = sizes
    n_s, nz, nx, ny = conc.shape
    n_e = measured.shape[0]
    n_k = measured.shape[1]
    fan = weight.shape[0]
    c1 = 1.5 / (nx * n_beam)
    c2 = 1.5 / (ny * n_det)
    blocks = nx // BLOCK
    step = nx // CHUNKS
    per_chunk = blocks // CHUNKS
    beam, det, slab = lax.axis_index("beam"), lax.axis_index("det"), lax.axis_index("slab")

    def load(chunk, z):
        rows = pl.ds(chunk * step, step)
        return pltpu.make_async_copy(conc.at[:, z, rows, :], c_buf.at[:, rows, z, :], in_sem.at[chunk, z])

    for chunk in range(CHUNKS):
        for z in range(nz):
            load(chunk, z).start()
    load_measured = pltpu.make_async_copy(measured, meas, meas_sem)
    load_measured.start()

    def beam_at(away):
        return lax.rem(beam + away, n_beam)

    def slab_at(away):
        return lax.rem(slab + away, n_slab)

    halo = (1, n_slab - 1)
    peers = [{"det": lax.rem(det + away, n_det)} for away in range(1, n_det)]
    for slab_away in range(n_slab):
        for beam_away in range(n_beam):
            if slab_away == 0 and beam_away == 0:
                continue
            if slab_away == 0 or slab_away in halo or beam_away == 0:
                peers.append({"beam": beam_at(beam_away), "slab": slab_at(slab_away)})
    barrier = pltpu.get_barrier_semaphore()
    for peer in peers:
        pl.semaphore_signal(barrier, inc=1, device_id=peer, device_id_type=MESH)

    def remote(src, dst, send, recv, device):
        return pltpu.make_async_remote_copy(
            src_ref=src, dst_ref=dst, send_sem=send, recv_sem=recv, device_id=device, device_id_type=MESH
        )

    def depth_copy(away):
        return remote(ra_send, ra_recv.at[away], ra_ss.at[away], ra_rs.at[away], {"det": lax.rem(det - away + n_det, n_det)})

    def column_copy(away):
        return remote(rc_send, rc_recv.at[away], rc_ss.at[away], rc_rs.at[away], {"det": lax.rem(det + away, n_det)})

    def beam_copy(away):
        slot = n_beam - away
        return remote(ud_send, ud_recv.at[slot], ud_ss.at[away], ud_rs.at[slot], {"beam": beam_at(away)})

    def line_copy(part, away):
        slot = (n_beam - away) % n_beam
        if part == 1:
            src, rows, target = x_buf.at[0, :, pl.ds(nz, nz), :], pl.ds(nz, nz), slab
        elif part == 0:
            src, rows, target = x_buf.at[0, :, pl.ds(2 * nz - REACH, REACH), :], pl.ds(nz - REACH, REACH), slab_at(1)
        else:
            src, rows, target = x_buf.at[0, :, pl.ds(nz, REACH), :], pl.ds(2 * nz, REACH), slab_at(n_slab - 1)
        return remote(
            src, x_buf.at[slot, :, rows, :], x_ss.at[part, away], x_rs.at[part, slot], {"beam": beam_at(away), "slab": target}
        )

    def slab_copy(away, receiving):
        source = slab_at(away) if receiving else slab
        rows = pl.ds(pl.multiple_of(source * nz, nz), nz)
        slot = away if receiving else n_slab - away
        return remote(
            xl.at[:, pl.ds(nz, nz), :], la.at[:, rows, :], la_ss.at[away], la_rs.at[slot], {"slab": slab_at(away)}
        )

    sigma = [[cross[s, index[e]] * c1 for e in range(n_e)] for s in range(n_s)]
    lam_near = [lam[s] * c2 for s in range(n_s)]
    lam_before = [lam[s] * (c2 / c1) for s in range(n_s)]

    def first(block, depth):
        depth = list(depth)
        absorb = []
        for part in range(BLOCK // 4):
            rows = pl.ds(block * BLOCK + part * 4, 4)
            c = [c_buf[s, rows] for s in range(n_s)]
            ab = lam_near[0] * c[0]
            for s in range(1, n_s):
                ab = ab + lam_near[s] * c[s]
            absorb.append(ab)
            for e in range(n_e):
                value = sigma[0][e] * c[0]
                for s in range(1, n_s):
                    value = value + sigma[s][e] * c[s]
                em[e, rows] = value
                for x in range(4):
                    inc[e, block * BLOCK + part * 4 + x] = jnp.exp(-depth[e])
                    depth[e] = depth[e] + value[x]
        pair = split_pair(jnp.concatenate(absorb, axis=0).reshape(BLOCK * nz, ny))
        hl[block] = pair
        ra_send[pl.ds(block, 1), :] = row_totals(pair)
        return tuple(depth)

    depth = (jnp.zeros((nz, ny), F32),) * n_e
    for chunk in range(CHUNKS):
        for z in range(nz):
            load(chunk, z).wait()
        depth = lax.fori_loop(chunk * per_chunk, (chunk + 1) * per_chunk, first, depth)
    for e in range(n_e):
        ud_send[e] = depth[e]

    pl.semaphore_wait(barrier, len(peers))
    for away in range(1, n_det):

        @pl.when(det - away >= 0)
        def _():
            depth_copy(away).start()

    for away in range(1, n_beam):
        beam_copy(away).start()

    for away in range(1, n_det):

        @pl.when(det + away >= n_det)
        def _():
            ra_recv[away] = jnp.zeros_like(ra_send)

        @pl.when(det - away < 0)
        def _():
            rc_recv[away] = jnp.zeros_like(rc_send)

    deep = lax.broadcasted_iota(jnp.int32, (2 * ny, ny), 0) % ny
    wide = lax.broadcasted_iota(jnp.int32, (2 * ny, ny), 1)
    beyond = jnp.where(deep > wide, 1.0, 0.0).astype(BF16)
    nearer_side = jnp.where(deep < wide, 1.0, 0.0).astype(BF16)

    def second(block, carry):
        path = jnp.dot(hl[block], beyond, preferred_element_type=F32)
        escape = jnp.exp(-path).reshape(BLOCK, nz, ny)
        rows = pl.ds(block * BLOCK, BLOCK)
        for e in range(n_e):
            light = inc[e, rows] * escape
            inc[e, rows] = light
            em[e, rows] = em[e, rows] * light
        return carry

    lax.fori_loop(0, blocks, second, 0)

    slices = lax.broadcasted_iota(jnp.int32, wt.shape, 0) - nz
    full = jnp.zeros(wt.shape, F32)
    for j in range(fan):
        tap = weight[j : j + 1, :].astype(F32)
        full = full + jnp.where(offset[...] + j == slices, tap, 0.0)
    wt[...] = full
    wx[...] = wt[pl.ds(pl.multiple_of(slab * nz, nz), 3 * nz), :]
    whole = wt[nz : nz + n_slab * nz, :]
    padded = jnp.concatenate([whole, jnp.zeros((128 - n_slab * nz, n_k), F32)], axis=0)
    wk[...] = jnp.transpose(padded)
    own = wx[nz : 2 * nz, :]
    for shift in range(2 * REACH + 1):
        other = wx[nz - REACH + shift : 2 * nz - REACH + shift, :]
        band[shift] = jnp.broadcast_to(jnp.sum(own * other, axis=1, keepdims=True), (nz, ny))
    load_measured.wait()
    for e in range(n_e):
        wm[e] = jnp.dot(own, meas[e], precision=HIGHEST, preferred_element_type=F32)

    for away in range(1, n_beam):
        beam_copy(away).wait_recv()
    upstream = jnp.zeros((n_e, nz, ny), F32)
    for slot in range(1, n_beam):
        upstream = upstream + jnp.where(beam + slot >= n_beam, 1.0, 0.0) * ud_recv[slot]
    up_buf[...] = jnp.exp(-upstream)

    for away in range(1, n_det):

        @pl.when(det + away < n_det)
        def _():
            depth_copy(away).wait_recv()

    downstream = ra_recv[1]
    for away in range(2, n_det):
        downstream = downstream + ra_recv[away]
    for r, piece in enumerate(spread(jnp.exp(-downstream))):
        dmp[r * BLOCK : (r + 1) * BLOCK] = piece.reshape(BLOCK, nz, ny)

    def third(block, sums):
        rows = pl.ds(block * BLOCK, BLOCK)
        damp = dmp[rows]
        return tuple(sums[e] + jnp.sum(em[e, rows] * damp, axis=0) for e in range(n_e))

    sums = lax.fori_loop(0, blocks, third, (jnp.zeros((nz, ny), F32),) * n_e)
    for e in range(n_e):
        x_buf[0, e, nz : 2 * nz] = sums[e] * up_buf[e]
    for away in range(n_beam):
        for part in (1, 0, 2):
            if part == 1 and away == 0:
                continue
            line_copy(part, away).start()

    def fourth(count, after):
        block = blocks - 1 - count
        after = list(after)
        for x in range(BLOCK - 1, -1, -1):
            row = block * BLOCK + x
            damp = dmp[row]
            for e in range(n_e):
                fluor = em[e, row] * damp
                inc[e, row] = inc[e, row] * damp - after[e]
                em[e, row] = fluor
                after[e] = after[e] + fluor
        return tuple(after)

    lax.fori_loop(0, blocks, fourth, (jnp.zeros((nz, ny), F32),) * n_e)

    for away in range(n_beam):
        for part in (1, 0, 2):
            if part == 1 and away == 0:
                continue
            line_copy(part, away).wait_recv()
    near = slice(nz - REACH, 2 * nz + REACH)
    extent = x_buf[0, :, near]
    for slot in range(1, n_beam):
        extent = extent + x_buf[slot, :, near]
    xl[:, near] = extent
    further = jnp.zeros((n_e, nz, ny), F32)
    for slot in range(1, n_beam):
        further = further + jnp.where(beam + slot < n_beam, 1.0, 0.0) * x_buf[slot, :, nz : 2 * nz]
    back = []
    for e in range(n_e):
        value = band[0] * xl[e, nz - REACH : 2 * nz - REACH]
        for shift in range(1, 2 * REACH + 1):
            value = value + band[shift] * xl[e, nz - REACH + shift : 2 * nz - REACH + shift]
        back.append(value * (1.0 / 1.5) - wm[e])
    lit = [back[e] * up_buf[e] for e in range(n_e)]

    def fifth(block, carry):
        rows = pl.ds(block * BLOCK, BLOCK)
        heavy = lit[0] * em[0, rows]
        for e in range(1, n_e):
            heavy = heavy + lit[e] * em[e, rows]
        pair = split_pair(heavy.reshape(BLOCK * nz, ny))
        hl[block] = pair
        rc_send[pl.ds(block, 1), :] = row_totals(pair)
        return carry

    lax.fori_loop(0, blocks, fifth, 0)
    for away in range(1, n_det):

        @pl.when(det + away < n_det)
        def _():
            column_copy(away).start()

    for away in range(1, n_slab):
        slab_copy(away, False).start()
    la[:, pl.ds(pl.multiple_of(slab * nz, nz), nz), :] = xl[:, nz : 2 * nz, :]
    shade = [back[e] * further[e] for e in range(n_e)]
    mix, less = [], []
    for s in range(n_s):
        pull = [cross[s, index[e]] for e in range(n_e)]
        mix.append([pull[e] * lit[e] for e in range(n_e)])
        value = pull[0] * shade[0]
        for e in range(1, n_e):
            value = value + pull[e] * shade[e]
        less.append(value)

    def sixth(block, carry):
        before = jnp.dot(hl[block], nearer_side, preferred_element_type=F32).reshape(BLOCK, nz, ny)
        for part in range(BLOCK // 4):
            rows = pl.ds(block * BLOCK + part * 4, 4)
            term = [inc[e, rows] for e in range(n_e)]
            for s in range(n_s):
                value = mix[s][0] * term[0]
                for e in range(1, n_e):
                    value = value + mix[s][e] * term[e]
                c_buf[s, rows] = value - less[s] - lam_before[s] * before[part * 4 : part * 4 + 4]
        return carry

    lax.fori_loop(0, blocks, sixth, 0)

    for away in range(1, n_slab):
        slab_copy(away, True).wait_recv()
    share = n_k // (n_beam * n_slab)
    mine = pl.ds(pl.multiple_of((beam * n_slab + slab) * share, share), share)
    for e in range(n_e):
        signal = jnp.dot(wk[mine, 0 : n_slab * nz], la[e], precision=HIGHEST, preferred_element_type=F32)
        resid[e] = signal * (1.0 / 1.5) - meas[e, mine]

    for away in range(1, n_det):

        @pl.when(det - away >= 0)
        def _():
            remote(rc_send, rc_recv.at[away], rc_ss.at[away], rc_rs.at[away], {"det": lax.rem(det + away, n_det)}).wait_recv()

    nearer = rc_recv[1]
    for away in range(2, n_det):
        nearer = nearer + rc_recv[away]
    for r, piece in enumerate(spread(nearer)):
        dmp[r * BLOCK : (r + 1) * BLOCK] = piece.reshape(BLOCK, nz, ny)

    def store(chunk, z):
        rows = pl.ds(chunk * step, step)
        return pltpu.make_async_copy(c_buf.at[:, rows, z, :], out.at[:, z, rows, :], out_sem.at[chunk, z])

    def seventh(block, carry):
        rows = pl.ds(block * BLOCK, BLOCK)
        shift = dmp[rows]
        for s in range(n_s):
            c_buf[s, rows] = c_buf[s, rows] - lam_before[s] * shift
        return carry

    for chunk in range(CHUNKS):
        lax.fori_loop(chunk * per_chunk, (chunk + 1) * per_chunk, seventh, 0)
        for z in range(nz):
            store(chunk, z).start()

    for away in range(1, n_det):

        @pl.when(det - away >= 0)
        def _():
            depth_copy(away).wait_send()

        @pl.when(det + away < n_det)
        def _():
            column_copy(away).wait_send()

    for away in range(1, n_beam):
        beam_copy(away).wait_send()
    for away in range(n_beam):
        for part in (1, 0, 2):
            if part == 1 and away == 0:
                continue
            line_copy(part, away).wait_send()
    for away in range(1, n_slab):
        slab_copy(away, False).wait_send()
    for chunk in range(CHUNKS):
        for z in range(nz):
            store(chunk, z).wait()


def solution(mesh):
    sizes = (mesh.shape["beam"], mesh.shape["det"], mesh.shape["slab"])
    n_beam, n_det, n_slab = sizes

    def shards(concentration, cross_section, line_attenuation, energy_index, fan_offset, fan_weight, measured):
        n_s, nz, nx, ny = concentration.shape
        n_e, n_k = measured.shape[0], measured.shape[1]
        share = n_k // (n_beam * n_slab)
        volume = pltpu.VMEM((n_e, nx, nz, ny), F32)
        compact = (nx * nz // 128, 128)
        dma = pltpu.SemaphoreType.DMA
        scratch = [
            pltpu.VMEM((n_s, nx, nz, ny), F32),
            volume,
            volume,
            pltpu.VMEM((nx, nz, ny), F32),
            pltpu.VMEM((nx // BLOCK, BLOCK * nz, 2 * ny), BF16),
            pltpu.VMEM((n_e, n_k, ny), F32),
            pltpu.VMEM(((n_slab + 2) * nz, n_k), F32),
            pltpu.VMEM((3 * nz, n_k), F32),
            pltpu.VMEM((n_k, 128), F32),
            pltpu.VMEM((2 * REACH + 1, nz, ny), F32),
            pltpu.VMEM((n_e, nz, ny), F32),
            pltpu.VMEM((n_e, nz, ny), F32),
            pltpu.VMEM(compact, F32),
            pltpu.VMEM((n_det, *compact), F32),
            pltpu.VMEM((n_e, nz, ny), F32),
            pltpu.VMEM((n_beam, n_e, nz, ny), F32),
            pltpu.VMEM((n_beam, n_e, 3 * nz, ny), F32),
            pltpu.VMEM((n_e, 3 * nz, ny), F32),
            pltpu.VMEM((n_e, n_slab * nz, ny), F32),
            pltpu.VMEM(compact, F32),
            pltpu.VMEM((n_det, *compact), F32),
            dma((CHUNKS, nz)),
            dma,
            dma((n_det,)),
            dma((n_det,)),
            dma((n_beam,)),
            dma((n_beam,)),
            dma((3, n_beam)),
            dma((3, n_beam)),
            dma((n_slab,)),
            dma((n_slab,)),
            dma((n_det,)),
            dma((n_det,)),
            dma((CHUNKS, nz)),
        ]
        smem = pl.BlockSpec(memory_space=pltpu.SMEM)
        vmem = pl.BlockSpec(memory_space=pltpu.VMEM)
        anywhere = pl.BlockSpec(memory_space=pl.ANY)
        return pl.pallas_call(
            functools.partial(kernel, sizes),
            out_shape=(
                jax.ShapeDtypeStruct(concentration.shape, F32),
                jax.ShapeDtypeStruct((n_e, share, ny), F32),
            ),
            in_specs=[anywhere, smem, smem, smem, vmem, vmem, anywhere],
            out_specs=(anywhere, vmem),
            scratch_shapes=scratch,
            compiler_params=pltpu.CompilerParams(
                collective_id=0, has_side_effects=True, vmem_limit_bytes=48 * 2**20
            ),
        )(
            concentration,
            cross_section,
            line_attenuation,
            energy_index,
            fan_offset.reshape(1, n_k),
            fan_weight.T,
            measured,
        )

    in_specs = (P(None, "slab", "beam", "det"), P(), P(), P(), P(), P(), P(None, None, "det"))
    out_specs = (P(None, "slab", "beam", "det"), P(None, ("beam", "slab"), "det"))
    return jax.shard_map(shards, mesh=mesh, in_specs=in_specs, out_specs=out_specs, check_vma=False)
```

time: 318 us -> 43.9 us (0.14); the launches traced: 312 us -> 43.7 us
  waiting for transfers between devices: 109 us -> 0 us
  other arithmetic: 91.1 us -> 0 us
  blocking collectives: 51.7 us -> 0 us
  Pallas kernels: 0 us -> 36 us
  local copies, waits for them, and re-layouts: 41.4 us -> 7.02 us
  between operations: 16.9 us -> 0.65 us
    psum x1 -> x0, waiting for transfers between devices: 109 us -> none  [shards(): signal = lax.psum(partial_signal, ('beam', 'slab'))]
    all_gather x4 -> x0, blocking collectives: 51.7 us -> none  [entering(): pieces = lax.all_gather(value, axis)]
    pallas_call x0 -> x1, Pallas kernels: none -> 36 us  [shards(): pl.pallas_call(functools.partial(kernel, sizes), out_shape=(jax.ShapeDtyp...]
    select_n x36 -> x0, other arithmetic: 29.4 us -> none  [lap(): return jnp.where(position < mine, longer, running)]
    sub x5 -> x0, other arithmetic: 18.8 us -> none  [the longest x3 11.3 us: shards(): result.append(accum - line_attenuation[species] * (1.5 / full_y) * before_y)]
    another operation x9 -> x0, other arithmetic: 17.2 us -> none
    reduce_sum x6 -> x0, other arithmetic: 16.5 us -> none  [the longest x1 6.25 us: shards(): line_sums = jnp.sum(fluor, axis=2)]
    another operation x5 -> x0, local copies, waits for them, and re-layouts: 13.8 us -> none
  transfers between devices with their start and end apart: 1 -> 0, of which waited for: 1 -> 0; matrix products, arithmetic and copies ran while one was open for 1% -> 0% of each run, Pallas kernels for 0% -> 0%
where the time goes in v1:
time: 43.9 us; the launch traced here: 43.7 us
  Pallas kernels  36 us (82%)
  local copies, waits for them, and re-layouts  7.02 us (16%)
  between operations  0.65 us (1%)
    pallas_call x1, Pallas kernels, shards(): pl.pallas_call(functools.partial(kernel, sizes), out_shape=(jax.ShapeDtyp...  36 us
    unnamed x14, local copies, waits for them, and re-layouts  7.02 us

profile of v1, /device:TPU:1, one launch (start us, length us, event | category | flops | bytes accessed | tf_op | source)
XLA Modules:
  0.0 43.7 jit_solution(17307739677564471298)
XLA Ops:
  0.6 0.0 copy-start
  0.6 1.0 %copy-done = f32[4,256,128]{2,1,0:T(8,128)S(1)} copy-done((f32[4,256,128]{2,1,0:T(8,128)S(1)}, f32[4,256,128]{2,1,0:T(8,128)}, u32[]{:S(2)}) %copy-start) | copy-done | bytes 524312
  1.7 0.0 copy-start.1
  1.7 0.7 %copy-done.1 = s32[256,4]{0,1:T(4,128)S(1)} copy-done((s32[256,4]{0,1:T(4,128)S(1)}, s32[256,4]{0,1:T(4,128)}, u32[]{:S(2)}) %copy-start.1) | copy-done | bytes 4120
  2.4 0.0 copy-start.2
  2.4 0.7 %copy-done.2 = f32[4,16]{1,0:T(4,128)S(1)} copy-done((f32[4,16]{1,0:T(4,128)S(1)}, f32[4,16]{1,0:T(4,128)}, u32[]{:S(2)}) %copy-start.2) | copy-done | bytes 280
  3.0 0.0 copy-start.3
  3.0 0.7 %copy-done.3 = s32[256]{0:T(256)S(1)} copy-done((s32[256]{0:T(256)S(1)}, s32[256]{0:T(256)}, u32[]{:S(2)}) %copy-start.3) | copy-done | bytes 1048
  3.7 0.0 copy-start.4
  3.7 0.7 %copy-done.4 = f32[4]{0:T(128)S(1)} copy-done((f32[4]{0:T(128)S(1)}, f32[4]{0:T(128)}, u32[]{:S(2)}) %copy-start.4) | copy-done | bytes 40
  4.4 0.0 copy-start.5
  4.4 0.7 %copy-done.5 = s32[4]{0:T(128)S(1)} copy-done((s32[4]{0:T(128)S(1)}, s32[4]{0:T(128)}, u32[]{:S(2)}) %copy-start.5) | copy-done | bytes 40
  5.0 36.0 %shard_map.86 = (f32[4,8,256,128]{3,2,1,0:T(8,128)S(1)}, f32[4,16,128]{2,1,0:T(8,128)S(1)}) custom-call(f32[4,8,256,128]{3,2,1,0:T(8,128)} %conc.1, f32[4,16]{1,0:T(4,128)S(1)} %copy-done.2, f32[4]{0:T(128)S(1)} %copy-done.4, s32[4]{0:T(128)S(1)} %copy-done.5, s32[1,256]{1,0:T(1,128)S(1)} %bitcast.3, s32[4,256]{1,0:T(4,128)S(1)} %bitcast.2, ...), custom_call_target="tpu_custom_call" | custom-call | tf_op jit(solution)/shard_map/pallas_call | solution.py:432
  41.1 2.0 %copy.11 = f32[4,8,256,128]{3,2,1,0:T(8,128)} copy(f32[4,8,256,128]{3,2,1,0:T(8,128)S(1)} %get-tuple-element.4) | data formatting | bytes 8388608
  43.1 0.6 %copy.12 = f32[4,16,128]{2,1,0:T(8,128)} copy(f32[4,16,128]{2,1,0:T(8,128)S(1)} %get-tuple-element.5) | data formatting | bytes 65536
Async XLA Ops:
  0.6 1.0 %copy-start = (f32[4,256,128]{2,1,0:T(8,128)S(1)}, f32[4,256,128]{2,1,0:T(8,128)}, u32[]{:S(2)}) copy-start(f32[4,256,128]{2,1,0:T(8,128)} %measured.1) | copy-start | bytes 1572868
  1.7 0.7 %copy-start.1 = (s32[256,4]{0,1:T(4,128)S(1)}, s32[256,4]{0,1:T(4,128)}, u32[]{:S(2)}) copy-start(s32[256,4]{0,1:T(4,128)} %param.12) | copy-start | bytes 12292
  2.4 0.7 %copy-start.2 = (f32[4,16]{1,0:T(4,128)S(1)}, f32[4,16]{1,0:T(4,128)}, u32[]{:S(2)}) copy-start(f32[4,16]{1,0:T(4,128)} %cross.1) | copy-start | bytes 772
  3.0 0.7 %copy-start.3 = (s32[256]{0:T(256)S(1)}, s32[256]{0:T(256)}, u32[]{:S(2)}) copy-start(s32[256]{0:T(256)} %param.11) | copy-start | bytes 3076
  3.7 0.7 %copy-start.4 = (f32[4]{0:T(128)S(1)}, f32[4]{0:T(128)}, u32[]{:S(2)}) copy-start(f32[4]{0:T(128)} %lam.1) | copy-start | bytes 52
  4.4 0.7 %copy-start.5 = (s32[4]{0:T(128)S(1)}, s32[4]{0:T(128)}, u32[]{:S(2)}) copy-start(s32[4]{0:T(128)} %index.1) | copy-start | bytes 52

commit v2 on v1

--- a/solution.py
+++ b/solution.py
@@ -36,16 +36,16 @@
 
 
 def kernel(
-    sizes, conc, cross, lam, index, offset, weight, measured, out, resid,
-    c_buf, em, inc, dmp, hl, meas, wt, wx, wk, band, wm, up_buf,
+    sizes, conc, cross_in, lam_in, index_in, offset_in, weight_in, measured, part_out, near_out, lam_out, resid,
+    cross, lam, index, offset, weight, c_buf, em, inc, dmp, hl, meas, wt, wx, wk, band, wm, up_buf,
     ra_send, ra_recv, ud_send, ud_recv, x_buf, xl, la, rc_send, rc_recv,
-    in_sem, meas_sem, ra_ss, ra_rs, ud_ss, ud_rs, x_ss, x_rs, la_ss, la_rs, rc_ss, rc_rs, out_sem,
+    in_sem, small_sem, meas_sem, ra_ss, ra_rs, ud_ss, ud_rs, x_ss, x_rs, la_ss, la_rs, rc_ss, rc_rs,
 ):
     n_beam, n_det, n_slab = sizes
     n_s, nz, nx, ny = conc.shape
     n_e = measured.shape[0]
     n_k = measured.shape[1]
-    fan = weight.shape[0]
+    fan = weight_in.shape[0]
     c1 = 1.5 / (nx * n_beam)
     c2 = 1.5 / (ny * n_det)
     blocks = nx // BLOCK
@@ -57,6 +57,10 @@
         rows = pl.ds(chunk * step, step)
         return pltpu.make_async_copy(conc.at[:, z, rows, :], c_buf.at[:, rows, z, :], in_sem.at[chunk, z])
 
+    pairs = ((cross_in, cross), (lam_in, lam), (index_in, index), (offset_in, offset), (weight_in, weight))
+    small = [pltpu.make_async_copy(src, dst, small_sem.at[n]) for n, (src, dst) in enumerate(pairs)]
+    for copy in small:
+        copy.start()
     for chunk in range(CHUNKS):
         for z in range(nz):
             load(chunk, z).start()
@@ -116,9 +120,17 @@
             xl.at[:, pl.ds(nz, nz), :], la.at[:, rows, :], la_ss.at[away], la_rs.at[slot], {"slab": slab_at(away)}
         )
 
+    for copy in small:
+        copy.wait()
     sigma = [[cross[s, index[e]] * c1 for e in range(n_e)] for s in range(n_s)]
     lam_near = [lam[s] * c2 for s in range(n_s)]
     lam_before = [lam[s] * (c2 / c1) for s in range(n_s)]
+
+    def compact_totals(dst, low, high):
+        total = row_totals(hl[low * step * nz : high * step * nz])
+        for r in range(high * per_chunk - low * per_chunk):
+            row = low * per_chunk + r
+            dst[row : row + 1, :] = total[:, r * 128 : (r + 1) * 128]
 
     def first(block, depth):
         depth = list(depth)
@@ -136,11 +148,11 @@
                     value = value + sigma[s][e] * c[s]
                 em[e, rows] = value
                 for x in range(4):
-                    inc[e, block * BLOCK + part * 4 + x] = jnp.exp(-depth[e])
-                    depth[e] = depth[e] + value[x]
-        pair = split_pair(jnp.concatenate(absorb, axis=0).reshape(BLOCK * nz, ny))
-        hl[block] = pair
-        ra_send[pl.ds(block, 1), :] = row_totals(pair)
+                    inc[e, block * BLOCK + part * 4 + x] = jnp.exp(depth[e])
+                    depth[e] = depth[e] - value[x]
+        hl[pl.ds(pl.multiple_of(block * BLOCK * nz, 128), BLOCK * nz)] = split_pair(
+            jnp.concatenate(absorb, axis=0).reshape(BLOCK * nz, ny)
+        )
         return tuple(depth)
 
     depth = (jnp.zeros((nz, ny), F32),) * n_e
@@ -148,6 +160,8 @@
         for z in range(nz):
             load(chunk, z).wait()
         depth = lax.fori_loop(chunk * per_chunk, (chunk + 1) * per_chunk, first, depth)
+        if chunk % 2:
+            compact_totals(ra_send, chunk - 1, chunk + 1)
     for e in range(n_e):
         ud_send[e] = depth[e]
 
@@ -173,20 +187,18 @@
 
     deep = lax.broadcasted_iota(jnp.int32, (2 * ny, ny), 0) % ny
     wide = lax.broadcasted_iota(jnp.int32, (2 * ny, ny), 1)
-    beyond = jnp.where(deep > wide, 1.0, 0.0).astype(BF16)
+    beyond = jnp.where(deep > wide, -1.0, 0.0).astype(BF16)
     nearer_side = jnp.where(deep < wide, 1.0, 0.0).astype(BF16)
 
-    def second(block, carry):
-        path = jnp.dot(hl[block], beyond, preferred_element_type=F32)
-        escape = jnp.exp(-path).reshape(BLOCK, nz, ny)
+    tile = BLOCK * nz
+    for block in range(blocks):
+        path = jnp.dot(hl[block * tile : (block + 1) * tile], beyond, preferred_element_type=F32)
+        escape = jnp.exp(path).reshape(BLOCK, nz, ny)
         rows = pl.ds(block * BLOCK, BLOCK)
         for e in range(n_e):
             light = inc[e, rows] * escape
             inc[e, rows] = light
             em[e, rows] = em[e, rows] * light
-        return carry
-
-    lax.fori_loop(0, blocks, second, 0)
 
     slices = lax.broadcasted_iota(jnp.int32, wt.shape, 0) - nz
     full = jnp.zeros(wt.shape, F32)
@@ -211,7 +223,7 @@
     upstream = jnp.zeros((n_e, nz, ny), F32)
     for slot in range(1, n_beam):
         upstream = upstream + jnp.where(beam + slot >= n_beam, 1.0, 0.0) * ud_recv[slot]
-    up_buf[...] = jnp.exp(-upstream)
+    up_buf[...] = jnp.exp(upstream)
 
     for away in range(1, n_det):
 
@@ -275,17 +287,14 @@
         back.append(value * (1.0 / 1.5) - wm[e])
     lit = [back[e] * up_buf[e] for e in range(n_e)]
 
-    def fifth(block, carry):
+    for block in range(blocks):
         rows = pl.ds(block * BLOCK, BLOCK)
         heavy = lit[0] * em[0, rows]
         for e in range(1, n_e):
             heavy = heavy + lit[e] * em[e, rows]
-        pair = split_pair(heavy.reshape(BLOCK * nz, ny))
-        hl[block] = pair
-        rc_send[pl.ds(block, 1), :] = row_totals(pair)
-        return carry
-
-    lax.fori_loop(0, blocks, fifth, 0)
+        pair = split_pair(heavy.reshape(tile, ny))
+        hl[block * tile : (block + 1) * tile] = pair
+        rc_send[block : block + 1, :] = row_totals(pair)
     for away in range(1, n_det):
 
         @pl.when(det + away < n_det)
@@ -305,8 +314,11 @@
             value = value + pull[e] * shade[e]
         less.append(value)
 
+    for block in range(blocks):
+        before = jnp.dot(hl[block * tile : (block + 1) * tile], nearer_side, preferred_element_type=F32)
+        dmp[block * BLOCK : (block + 1) * BLOCK] = before.reshape(BLOCK, nz, ny)
+
     def sixth(block, carry):
-        before = jnp.dot(hl[block], nearer_side, preferred_element_type=F32).reshape(BLOCK, nz, ny)
         for part in range(BLOCK // 4):
             rows = pl.ds(block * BLOCK + part * 4, 4)
             term = [inc[e, rows] for e in range(n_e)]
@@ -314,7 +326,7 @@
                 value = mix[s][0] * term[0]
                 for e in range(1, n_e):
                     value = value + mix[s][e] * term[e]
-                c_buf[s, rows] = value - less[s] - lam_before[s] * before[part * 4 : part * 4 + 4]
+                part_out[s, rows] = value - less[s] - lam_before[s] * dmp[rows]
         return carry
 
     lax.fori_loop(0, blocks, sixth, 0)
@@ -336,24 +348,9 @@
     nearer = rc_recv[1]
     for away in range(2, n_det):
         nearer = nearer + rc_recv[away]
-    for r, piece in enumerate(spread(nearer)):
-        dmp[r * BLOCK : (r + 1) * BLOCK] = piece.reshape(BLOCK, nz, ny)
-
-    def store(chunk, z):
-        rows = pl.ds(chunk * step, step)
-        return pltpu.make_async_copy(c_buf.at[:, rows, z, :], out.at[:, z, rows, :], out_sem.at[chunk, z])
-
-    def seventh(block, carry):
-        rows = pl.ds(block * BLOCK, BLOCK)
-        shift = dmp[rows]
-        for s in range(n_s):
-            c_buf[s, rows] = c_buf[s, rows] - lam_before[s] * shift
-        return carry
-
-    for chunk in range(CHUNKS):
-        lax.fori_loop(chunk * per_chunk, (chunk + 1) * per_chunk, seventh, 0)
-        for z in range(nz):
-            store(chunk, z).start()
+    near_out[...] = nearer
+    for s in range(n_s):
+        lam_out[s] = jnp.full((nz, ny), lam_before[s], F32)
 
     for away in range(1, n_det):
 
@@ -374,6 +371,26 @@
             line_copy(part, away).wait_send()
     for away in range(1, n_slab):
         slab_copy(away, False).wait_send()
+
+
+def finish(part, near, lam_before, resid_in, out, resid, buf, out_sem):
+    n_s, nx, nz, ny = part.shape
+    step = nx // CHUNKS
+    resid[...] = resid_in[...]
+    pieces = spread(near[...])
+
+    def store(chunk, z):
+        rows = pl.ds(chunk * step, step)
+        return pltpu.make_async_copy(buf.at[:, rows, z, :], out.at[:, z, rows, :], out_sem.at[chunk, z])
+
+    for chunk in range(CHUNKS):
+        for block in range(chunk * step // BLOCK, (chunk + 1) * step // BLOCK):
+            rows = slice(block * BLOCK, (block + 1) * BLOCK)
+            shift = pieces[block].reshape(BLOCK, nz, ny)
+            for s in range(n_s):
+                buf[s, rows] = part[s, rows] - lam_before[s] * shift
+        for z in range(nz):
+            store(chunk, z).start()
     for chunk in range(CHUNKS):
         for z in range(nz):
             store(chunk, z).wait()
@@ -391,11 +408,16 @@
         compact = (nx * nz // 128, 128)
         dma = pltpu.SemaphoreType.DMA
         scratch = [
+            pltpu.SMEM(cross_section.shape, F32),
+            pltpu.SMEM(line_attenuation.shape, F32),
+            pltpu.SMEM(energy_index.shape, jnp.int32),
+            pltpu.VMEM((1, n_k), jnp.int32),
+            pltpu.VMEM((fan_weight.shape[1], n_k), jnp.int32),
             pltpu.VMEM((n_s, nx, nz, ny), F32),
             volume,
             volume,
             pltpu.VMEM((nx, nz, ny), F32),
-            pltpu.VMEM((nx // BLOCK, BLOCK * nz, 2 * ny), BF16),
+            pltpu.VMEM((nx * nz, 2 * ny), BF16),
             pltpu.VMEM((n_e, n_k, ny), F32),
             pltpu.VMEM(((n_slab + 2) * nz, n_k), F32),
             pltpu.VMEM((3 * nz, n_k), F32),
@@ -413,6 +435,7 @@
             pltpu.VMEM(compact, F32),
             pltpu.VMEM((n_det, *compact), F32),
             dma((CHUNKS, nz)),
+            dma((5,)),
             dma,
             dma((n_det,)),
             dma((n_det,)),
@@ -424,32 +447,49 @@
             dma((n_slab,)),
             dma((n_det,)),
             dma((n_det,)),
-            dma((CHUNKS, nz)),
         ]
-        smem = pl.BlockSpec(memory_space=pltpu.SMEM)
+        hbm = pl.BlockSpec(memory_space=pltpu.HBM)
         vmem = pl.BlockSpec(memory_space=pltpu.VMEM)
-        anywhere = pl.BlockSpec(memory_space=pl.ANY)
-        return pl.pallas_call(
+        share_shape = (n_e, share, ny)
+        passed = pl.pallas_call(
             functools.partial(kernel, sizes),
             out_shape=(
-                jax.ShapeDtypeStruct(concentration.shape, F32),
-                jax.ShapeDtypeStruct((n_e, share, ny), F32),
+                pltpu.VMEM((n_s, nx, nz, ny), F32),
+                pltpu.VMEM(compact, F32),
+                pltpu.VMEM((n_s, nz, ny), F32),
+                pltpu.VMEM(share_shape, F32),
             ),
-            in_specs=[anywhere, smem, smem, smem, vmem, vmem, anywhere],
-            out_specs=(anywhere, vmem),
+            in_specs=[hbm] * 7,
+            out_specs=(vmem,) * 4,
             scratch_shapes=scratch,
             compiler_params=pltpu.CompilerParams(
-                collective_id=0, has_side_effects=True, vmem_limit_bytes=48 * 2**20
+                collective_id=0, has_side_effects=True, vmem_limit_bytes=28 * 2**20
             ),
         )(
-            concentration,
-            cross_section,
-            line_attenuation,
-            energy_index,
-            fan_offset.reshape(1, n_k),
-            fan_weight.T,
-            measured,
+            *(
+                pltpu.with_memory_space_constraint(array, pltpu.HBM)
+                for array in (
+                    concentration,
+                    cross_section,
+                    line_attenuation,
+                    energy_index,
+                    fan_offset.reshape(1, n_k),
+                    fan_weight.T,
+                    measured,
+                )
+            )
         )
+        return pl.pallas_call(
+            finish,
+            out_shape=(
+                jax.ShapeDtypeStruct(concentration.shape, F32),
+                jax.ShapeDtypeStruct(share_shape, F32),
+            ),
+            in_specs=[vmem] * 4,
+            out_specs=(hbm, vmem),
+            scratch_shapes=[pltpu.VMEM((n_s, nx, nz, ny), F32), dma((CHUNKS, nz))],
+            compiler_params=pltpu.CompilerParams(vmem_limit_bytes=16 * 2**20),
+        )(*passed)
 
     in_specs = (P(None, "slab", "beam", "det"), P(), P(), P(), P(), P(), P(None, None, "det"))
     out_specs = (P(None, "slab", "beam", "det"), P(None, ("beam", "slab"), "det"))

time: 43.9 us -> 31.8 us (0.72)
  local copies, waits for them, and re-layouts: 7.02 us -> 0 us
  Pallas kernels: 36 us -> 31.1 us
    unnamed x14 -> x0, local copies, waits for them, and re-layouts: 7.02 us -> none
    pallas_call x1 -> x2, Pallas kernels: 36 us -> 31.1 us  [the longest x1 27.9 us: shards(): pl.pallas_call(functools.partial(kernel, sizes), out_shape=(pltpu.VMEM((n...]
where the time goes in v2:
time: 31.8 us; the launch traced here: 31.7 us
  Pallas kernels  31.1 us (98%)
  between operations  0.64 us (2%)
    pallas_call x1, Pallas kernels, shards(): pl.pallas_call(functools.partial(kernel, sizes), out_shape=(pltpu.VMEM((n...  27.9 us
    pallas_call x1, Pallas kernels, shards(): pl.pallas_call(finish, out_shape=(jax.ShapeDtypeStruct(concentration.shap...  3.14 us

profile of v2, /device:TPU:1, one launch (start us, length us, event | category | flops | bytes accessed | tf_op | source)
XLA Modules:
  0.0 31.7 jit_solution(6614821385927290752)
XLA Ops:
  0.6 27.9 %shard_map.86 = (f32[4,256,8,128]{3,2,1,0:T(8,128)S(1)}, f32[16,128]{1,0:T(8,128)S(1)}, f32[4,8,128]{2,1,0:T(8,128)S(1)}, f32[4,16,128]{2,1,0:T(8,128)S(1)}) custom-call(f32[4,8,256,128]{3,2,1,0:T(8,128)} %conc.1, f32[4,16]{1,0:T(4,128)} %cross_in.1, f32[4]{0:T(128)} %lam_in.1, s32[4]{0:T(128)} %index_in.1, s32[1,256]{1,0:T(1,128)} %bitcast.3, ...), custom_call_target="tpu_custom_call" | custom-call | tf_op jit(solution)/shard_map/pallas_call | solution.py:454
  28.6 3.1 %shard_map.87 = (f32[4,8,256,128]{3,2,1,0:T(8,128)}, f32[4,16,128]{2,1,0:T(8,128)}) custom-call(f32[4,256,8,128]{3,2,1,0:T(8,128)S(1)} %get-tuple-element.6.part, f32[16,128]{1,0:T(8,128)S(1)} %get-tuple-element.7.near, f32[4,8,128]{2,1,0:T(8,128)S(1)} %get-tuple-element.8.lam_before, f32[4,16,128]{2,1,0:T(8,128)S(1)} %get-tuple-element.9.resid_in), custom_call_target="tpu_custom_call" | custom-call | tf_op jit(solution)/shard_map/pallas_call | solution.py:482

commit v3 on v2

--- a/solution.py
+++ b/solution.py
@@ -11,7 +11,8 @@
 F32 = jnp.float32
 BF16 = jnp.bfloat16
 HIGHEST = lax.Precision.HIGHEST
-CHUNKS = 4
+CHUNKS = 2
+STORES = 4
 BLOCK = 16
 REACH = 3
 
@@ -112,6 +113,9 @@
             src, x_buf.at[slot, :, rows, :], x_ss.at[part, away], x_rs.at[part, slot], {"beam": beam_at(away), "slab": target}
         )
 
+    order = sorted(range(n_beam), key=lambda away: abs(2 * away - n_beam))
+    lines = [(part, away) for away in order for part in (0, 2)] + [(1, away) for away in order if away]
+
     def slab_copy(away, receiving):
         source = slab_at(away) if receiving else slab
         rows = pl.ds(pl.multiple_of(source * nz, nz), nz)
@@ -126,22 +130,34 @@
     lam_near = [lam[s] * c2 for s in range(n_s)]
     lam_before = [lam[s] * (c2 / c1) for s in range(n_s)]
 
-    def compact_totals(dst, low, high):
-        total = row_totals(hl[low * step * nz : high * step * nz])
-        for r in range(high * per_chunk - low * per_chunk):
-            row = low * per_chunk + r
-            dst[row : row + 1, :] = total[:, r * 128 : (r + 1) * 128]
+    tile = BLOCK * nz
+
+    def totals_of(value, block, dst):
+        pair = split_pair(value.reshape(tile, ny))
+        hl[block * tile : (block + 1) * tile] = pair
+        dst[block : block + 1, :] = row_totals(pair)
+
+    for chunk in range(CHUNKS):
+        for z in range(nz):
+            load(chunk, z).wait()
+        for block in range(chunk * per_chunk, (chunk + 1) * per_chunk):
+            rows = pl.ds(block * BLOCK, BLOCK)
+            absorb = lam_near[0] * c_buf[0, rows]
+            for s in range(1, n_s):
+                absorb = absorb + lam_near[s] * c_buf[s, rows]
+            totals_of(absorb, block, ra_send)
+    pl.semaphore_wait(barrier, len(peers))
+    for away in range(1, n_det):
+
+        @pl.when(det - away >= 0)
+        def _():
+            depth_copy(away).start()
 
     def first(block, depth):
         depth = list(depth)
-        absorb = []
         for part in range(BLOCK // 4):
             rows = pl.ds(block * BLOCK + part * 4, 4)
             c = [c_buf[s, rows] for s in range(n_s)]
-            ab = lam_near[0] * c[0]
-            for s in range(1, n_s):
-                ab = ab + lam_near[s] * c[s]
-            absorb.append(ab)
             for e in range(n_e):
                 value = sigma[0][e] * c[0]
                 for s in range(1, n_s):
@@ -150,28 +166,11 @@
                 for x in range(4):
                     inc[e, block * BLOCK + part * 4 + x] = jnp.exp(depth[e])
                     depth[e] = depth[e] - value[x]
-        hl[pl.ds(pl.multiple_of(block * BLOCK * nz, 128), BLOCK * nz)] = split_pair(
-            jnp.concatenate(absorb, axis=0).reshape(BLOCK * nz, ny)
-        )
         return tuple(depth)
 
-    depth = (jnp.zeros((nz, ny), F32),) * n_e
-    for chunk in range(CHUNKS):
-        for z in range(nz):
-            load(chunk, z).wait()
-        depth = lax.fori_loop(chunk * per_chunk, (chunk + 1) * per_chunk, first, depth)
-        if chunk % 2:
-            compact_totals(ra_send, chunk - 1, chunk + 1)
+    depth = lax.fori_loop(0, blocks, first, (jnp.zeros((nz, ny), F32),) * n_e)
     for e in range(n_e):
         ud_send[e] = depth[e]
-
-    pl.semaphore_wait(barrier, len(peers))
-    for away in range(1, n_det):
-
-        @pl.when(det - away >= 0)
-        def _():
-            depth_copy(away).start()
-
     for away in range(1, n_beam):
         beam_copy(away).start()
 
@@ -190,7 +189,6 @@
     beyond = jnp.where(deep > wide, -1.0, 0.0).astype(BF16)
     nearer_side = jnp.where(deep < wide, 1.0, 0.0).astype(BF16)
 
-    tile = BLOCK * nz
     for block in range(blocks):
         path = jnp.dot(hl[block * tile : (block + 1) * tile], beyond, preferred_element_type=F32)
         escape = jnp.exp(path).reshape(BLOCK, nz, ny)
@@ -245,11 +243,8 @@
     sums = lax.fori_loop(0, blocks, third, (jnp.zeros((nz, ny), F32),) * n_e)
     for e in range(n_e):
         x_buf[0, e, nz : 2 * nz] = sums[e] * up_buf[e]
-    for away in range(n_beam):
-        for part in (1, 0, 2):
-            if part == 1 and away == 0:
-                continue
-            line_copy(part, away).start()
+    for part, away in lines:
+        line_copy(part, away).start()
 
     def fourth(count, after):
         block = blocks - 1 - count
@@ -266,11 +261,8 @@
 
     lax.fori_loop(0, blocks, fourth, (jnp.zeros((nz, ny), F32),) * n_e)
 
-    for away in range(n_beam):
-        for part in (1, 0, 2):
-            if part == 1 and away == 0:
-                continue
-            line_copy(part, away).wait_recv()
+    for part, away in lines:
+        line_copy(part, away).wait_recv()
     near = slice(nz - REACH, 2 * nz + REACH)
     extent = x_buf[0, :, near]
     for slot in range(1, n_beam):
@@ -292,9 +284,7 @@
         heavy = lit[0] * em[0, rows]
         for e in range(1, n_e):
             heavy = heavy + lit[e] * em[e, rows]
-        pair = split_pair(heavy.reshape(tile, ny))
-        hl[block * tile : (block + 1) * tile] = pair
-        rc_send[block : block + 1, :] = row_totals(pair)
+        totals_of(heavy, block, rc_send)
     for away in range(1, n_det):
 
         @pl.when(det + away < n_det)
@@ -364,18 +354,15 @@
 
     for away in range(1, n_beam):
         beam_copy(away).wait_send()
-    for away in range(n_beam):
-        for part in (1, 0, 2):
-            if part == 1 and away == 0:
-                continue
-            line_copy(part, away).wait_send()
+    for part, away in lines:
+        line_copy(part, away).wait_send()
     for away in range(1, n_slab):
         slab_copy(away, False).wait_send()
 
 
 def finish(part, near, lam_before, resid_in, out, resid, buf, out_sem):
     n_s, nx, nz, ny = part.shape
-    step = nx // CHUNKS
+    step = nx // STORES
     resid[...] = resid_in[...]
     pieces = spread(near[...])
 
@@ -383,7 +370,7 @@
         rows = pl.ds(chunk * step, step)
         return pltpu.make_async_copy(buf.at[:, rows, z, :], out.at[:, z, rows, :], out_sem.at[chunk, z])
 
-    for chunk in range(CHUNKS):
+    for chunk in range(STORES):
         for block in range(chunk * step // BLOCK, (chunk + 1) * step // BLOCK):
             rows = slice(block * BLOCK, (block + 1) * BLOCK)
             shift = pieces[block].reshape(BLOCK, nz, ny)
@@ -391,7 +378,7 @@
                 buf[s, rows] = part[s, rows] - lam_before[s] * shift
         for z in range(nz):
             store(chunk, z).start()
-    for chunk in range(CHUNKS):
+    for chunk in range(STORES):
         for z in range(nz):
             store(chunk, z).wait()
 
@@ -434,7 +421,7 @@
             pltpu.VMEM((n_e, n_slab * nz, ny), F32),
             pltpu.VMEM(compact, F32),
             pltpu.VMEM((n_det, *compact), F32),
-            dma((CHUNKS, nz)),
+            dma((STORES, nz)),
             dma((5,)),
             dma,
             dma((n_det,)),
@@ -487,7 +474,7 @@
             ),
             in_specs=[vmem] * 4,
             out_specs=(hbm, vmem),
-            scratch_shapes=[pltpu.VMEM((n_s, nx, nz, ny), F32), dma((CHUNKS, nz))],
+            scratch_shapes=[pltpu.VMEM((n_s, nx, nz, ny), F32), dma((STORES, nz))],
             compiler_params=pltpu.CompilerParams(vmem_limit_bytes=16 * 2**20),
         )(*passed)
 

time: 31.8 us -> 31 us (0.975)
  Pallas kernels: 31.1 us -> 30.3 us
    pallas_call x1, Pallas kernels: 27.9 us -> 27.1 us  [shards(): pl.pallas_call(functools.partial(kernel, sizes), out_shape=(pltpu.VMEM((n...]
where the time goes in v3:
time: 31 us; the launch traced here: 30.9 us
  Pallas kernels  30.3 us (98%)
  between operations  0.64 us (2%)
    pallas_call x1, Pallas kernels, shards(): pl.pallas_call(functools.partial(kernel, sizes), out_shape=(pltpu.VMEM((n...  27.1 us
    pallas_call x1, Pallas kernels, shards(): pl.pallas_call(finish, out_shape=(jax.ShapeDtypeStruct(concentration.shap...  3.14 us

profile of v3, /device:TPU:1, one launch (start us, length us, event | category | flops | bytes accessed | tf_op | source)
XLA Modules:
  0.0 30.9 jit_solution(8363886066879845680)
XLA Ops:
  0.6 27.1 %shard_map.86 = (f32[4,256,8,128]{3,2,1,0:T(8,128)S(1)}, f32[16,128]{1,0:T(8,128)S(1)}, f32[4,8,128]{2,1,0:T(8,128)S(1)}, f32[4,16,128]{2,1,0:T(8,128)S(1)}) custom-call(f32[4,8,256,128]{3,2,1,0:T(8,128)} %conc.1, f32[4,16]{1,0:T(4,128)} %cross_in.1, f32[4]{0:T(128)} %lam_in.1, s32[4]{0:T(128)} %index_in.1, s32[1,256]{1,0:T(1,128)} %bitcast.3, ...), custom_call_target="tpu_custom_call" | custom-call | tf_op jit(solution)/shard_map/pallas_call | solution.py:441
  27.7 3.1 %shard_map.87 = (f32[4,8,256,128]{3,2,1,0:T(8,128)}, f32[4,16,128]{2,1,0:T(8,128)}) custom-call(f32[4,256,8,128]{3,2,1,0:T(8,128)S(1)} %get-tuple-element.6.part, f32[16,128]{1,0:T(8,128)S(1)} %get-tuple-element.7.near, f32[4,8,128]{2,1,0:T(8,128)S(1)} %get-tuple-element.8.lam_before, f32[4,16,128]{2,1,0:T(8,128)S(1)} %get-tuple-element.9.resid_in), custom_call_target="tpu_custom_call" | custom-call | tf_op jit(solution)/shard_map/pallas_call | solution.py:469

commit v4 on v3

--- a/solution.py
+++ b/solution.py
@@ -40,7 +40,7 @@
     sizes, conc, cross_in, lam_in, index_in, offset_in, weight_in, measured, part_out, near_out, lam_out, resid,
     cross, lam, index, offset, weight, c_buf, em, inc, dmp, hl, meas, wt, wx, wk, band, wm, up_buf,
     ra_send, ra_recv, ud_send, ud_recv, x_buf, xl, la, rc_send, rc_recv,
-    in_sem, small_sem, meas_sem, ra_ss, ra_rs, ud_ss, ud_rs, x_ss, x_rs, la_ss, la_rs, rc_ss, rc_rs,
+    in_sem, small_sem, meas_sem, ra_ss, ra_rs, ud_ss, ud_rs, x_ss, x_rs, la_ss, la_rs, rc_ss, rc_rs, relay_one, relay_two,
 ):
     n_beam, n_det, n_slab = sizes
     n_s, nz, nx, ny = conc.shape
@@ -74,17 +74,29 @@
     def slab_at(away):
         return lax.rem(slab + away, n_slab)
 
-    halo = (1, n_slab - 1)
-    peers = [{"det": lax.rem(det + away, n_det)} for away in range(1, n_det)]
-    for slab_away in range(n_slab):
-        for beam_away in range(n_beam):
-            if slab_away == 0 and beam_away == 0:
-                continue
-            if slab_away == 0 or slab_away in halo or beam_away == 0:
-                peers.append({"beam": beam_at(beam_away), "slab": slab_at(slab_away)})
+    cores = 2
+    deep_chips = n_beam // cores
+    chips = deep_chips * n_slab
+    chip, core = slab * deep_chips + beam // cores, lax.rem(beam, cores)
+
+    def chip_at(away, core_at):
+        there = lax.rem(chip + away, chips)
+        return {"beam": lax.rem(there, deep_chips) * cores + core_at, "slab": there // deep_chips}
+
+    near = [{"beam": beam - core + 1 - core}] + [chip_at(away, c) for away in (1, chips - 1) for c in range(cores)]
     barrier = pltpu.get_barrier_semaphore()
-    for peer in peers:
+    for away in range(1, n_det):
+
+        @pl.when(det + away < n_det)
+        def _():
+            pl.semaphore_signal(barrier, inc=1, device_id={"det": lax.rem(det + away, n_det)}, device_id_type=MESH)
+
+    for peer in near:
         pl.semaphore_signal(barrier, inc=1, device_id=peer, device_id_type=MESH)
+
+    def relay(sem):
+        for away in (1, chips - 1):
+            pl.semaphore_signal(sem, inc=1, device_id=chip_at(away, core), device_id_type=MESH)
 
     def remote(src, dst, send, recv, device):
         return pltpu.make_async_remote_copy(
@@ -146,12 +158,14 @@
             for s in range(1, n_s):
                 absorb = absorb + lam_near[s] * c_buf[s, rows]
             totals_of(absorb, block, ra_send)
-    pl.semaphore_wait(barrier, len(peers))
+    pl.semaphore_wait(barrier, det + len(near))
     for away in range(1, n_det):
 
         @pl.when(det - away >= 0)
         def _():
             depth_copy(away).start()
+
+    relay(relay_one)
 
     def first(block, depth):
         depth = list(depth)
@@ -173,6 +187,8 @@
         ud_send[e] = depth[e]
     for away in range(1, n_beam):
         beam_copy(away).start()
+    pl.semaphore_wait(relay_one, 2)
+    relay(relay_two)
 
     for away in range(1, n_det):
 
@@ -243,6 +259,7 @@
     sums = lax.fori_loop(0, blocks, third, (jnp.zeros((nz, ny), F32),) * n_e)
     for e in range(n_e):
         x_buf[0, e, nz : 2 * nz] = sums[e] * up_buf[e]
+    pl.semaphore_wait(relay_two, 2)
     for part, away in lines:
         line_copy(part, away).start()
 
@@ -263,11 +280,11 @@
 
     for part, away in lines:
         line_copy(part, away).wait_recv()
-    near = slice(nz - REACH, 2 * nz + REACH)
-    extent = x_buf[0, :, near]
+    middle = slice(nz - REACH, 2 * nz + REACH)
+    extent = x_buf[0, :, middle]
     for slot in range(1, n_beam):
-        extent = extent + x_buf[slot, :, near]
-    xl[:, near] = extent
+        extent = extent + x_buf[slot, :, middle]
+    xl[:, middle] = extent
     further = jnp.zeros((n_e, nz, ny), F32)
     for slot in range(1, n_beam):
         further = further + jnp.where(beam + slot < n_beam, 1.0, 0.0) * x_buf[slot, :, nz : 2 * nz]
@@ -434,6 +451,8 @@
             dma((n_slab,)),
             dma((n_det,)),
             dma((n_det,)),
+            pltpu.SemaphoreType.REGULAR,
+            pltpu.SemaphoreType.REGULAR,
         ]
         hbm = pl.BlockSpec(memory_space=pltpu.HBM)
         vmem = pl.BlockSpec(memory_space=pltpu.VMEM)

time: 31 us -> 30.3 us (0.977)
  Pallas kernels: 30.3 us -> 29.6 us
    pallas_call x1, Pallas kernels: 27.1 us -> 26.4 us  [shards(): pl.pallas_call(functools.partial(kernel, sizes), out_shape=(pltpu.VMEM((n...]
where the time goes in v4:
time: 30.3 us; the launch traced here: 30.2 us
  Pallas kernels  29.6 us (98%)
  between operations  0.64 us (2%)
    pallas_call x1, Pallas kernels, shards(): pl.pallas_call(functools.partial(kernel, sizes), out_shape=(pltpu.VMEM((n...  26.4 us
    pallas_call x1, Pallas kernels, shards(): pl.pallas_call(finish, out_shape=(jax.ShapeDtypeStruct(concentration.shap...  3.14 us

profile of v4, /device:TPU:1, one launch (start us, length us, event | category | flops | bytes accessed | tf_op | source)
XLA Modules:
  0.0 30.2 jit_solution(7432612736801203865)
XLA Ops:
  0.6 26.4 %shard_map.86 = (f32[4,256,8,128]{3,2,1,0:T(8,128)S(1)}, f32[16,128]{1,0:T(8,128)S(1)}, f32[4,8,128]{2,1,0:T(8,128)S(1)}, f32[4,16,128]{2,1,0:T(8,128)S(1)}) custom-call(f32[4,8,256,128]{3,2,1,0:T(8,128)} %conc.1, f32[4,16]{1,0:T(4,128)} %cross_in.1, f32[4]{0:T(128)} %lam_in.1, s32[4]{0:T(128)} %index_in.1, s32[1,256]{1,0:T(1,128)} %bitcast.3, ...), custom_call_target="tpu_custom_call" | custom-call | tf_op jit(solution)/shard_map/pallas_call | solution.py:460
  27.1 3.1 %shard_map.87 = (f32[4,8,256,128]{3,2,1,0:T(8,128)}, f32[4,16,128]{2,1,0:T(8,128)}) custom-call(f32[4,256,8,128]{3,2,1,0:T(8,128)S(1)} %get-tuple-element.6.part, f32[16,128]{1,0:T(8,128)S(1)} %get-tuple-element.7.near, f32[4,8,128]{2,1,0:T(8,128)S(1)} %get-tuple-element.8.lam_before, f32[4,16,128]{2,1,0:T(8,128)S(1)} %get-tuple-element.9.resid_in), custom_call_target="tpu_custom_call" | custom-call | tf_op jit(solution)/shard_map/pallas_call | solution.py:488

commit v5 on v4

--- a/solution.py
+++ b/solution.py
@@ -40,7 +40,7 @@
     sizes, conc, cross_in, lam_in, index_in, offset_in, weight_in, measured, part_out, near_out, lam_out, resid,
     cross, lam, index, offset, weight, c_buf, em, inc, dmp, hl, meas, wt, wx, wk, band, wm, up_buf,
     ra_send, ra_recv, ud_send, ud_recv, x_buf, xl, la, rc_send, rc_recv,
-    in_sem, small_sem, meas_sem, ra_ss, ra_rs, ud_ss, ud_rs, x_ss, x_rs, la_ss, la_rs, rc_ss, rc_rs, relay_one, relay_two,
+    in_sem, small_sem, meas_sem, ra_ss, ra_rs, ud_ss, ud_rs, x_ss, x_rs, la_ss, la_rs, rc_ss, rc_rs, relays,
 ):
     n_beam, n_det, n_slab = sizes
     n_s, nz, nx, ny = conc.shape
@@ -80,10 +80,11 @@
     chip, core = slab * deep_chips + beam // cores, lax.rem(beam, cores)
 
     def chip_at(away, core_at):
-        there = lax.rem(chip + away, chips)
+        there = lax.rem(chip + away + chips, chips)
         return {"beam": lax.rem(there, deep_chips) * cores + core_at, "slab": there // deep_chips}
 
-    near = [{"beam": beam - core + 1 - core}] + [chip_at(away, c) for away in (1, chips - 1) for c in range(cores)]
+    has = {-1: chip > 0, 1: chip < chips - 1}
+    beside = jnp.where(has[-1], 1, 0) + jnp.where(has[1], 1, 0)
     barrier = pltpu.get_barrier_semaphore()
     for away in range(1, n_det):
 
@@ -91,12 +92,24 @@
         def _():
             pl.semaphore_signal(barrier, inc=1, device_id={"det": lax.rem(det + away, n_det)}, device_id_type=MESH)
 
-    for peer in near:
-        pl.semaphore_signal(barrier, inc=1, device_id=peer, device_id_type=MESH)
-
-    def relay(sem):
-        for away in (1, chips - 1):
-            pl.semaphore_signal(sem, inc=1, device_id=chip_at(away, core), device_id_type=MESH)
+    other_core = {"beam": beam + 1 - 2 * core}
+    pl.semaphore_signal(barrier, inc=1, device_id=other_core, device_id_type=MESH)
+    for away in (-1, 1):
+
+        @pl.when(has[away])
+        def _():
+            for c in range(cores):
+                pl.semaphore_signal(barrier, inc=1, device_id=chip_at(away, c), device_id_type=MESH)
+
+    def tell(turn):
+        for away in (-1, 1):
+
+            @pl.when(has[away])
+            def _():
+                pl.semaphore_signal(relays.at[turn], inc=1, device_id=chip_at(away, core), device_id_type=MESH)
+
+    def hear(turn):
+        pl.semaphore_wait(relays.at[turn], beside)
 
     def remote(src, dst, send, recv, device):
         return pltpu.make_async_remote_copy(
@@ -158,14 +171,14 @@
             for s in range(1, n_s):
                 absorb = absorb + lam_near[s] * c_buf[s, rows]
             totals_of(absorb, block, ra_send)
-    pl.semaphore_wait(barrier, det + len(near))
+    pl.semaphore_wait(barrier, det + 1 + cores * beside)
     for away in range(1, n_det):
 
         @pl.when(det - away >= 0)
         def _():
             depth_copy(away).start()
 
-    relay(relay_one)
+    tell(0)
 
     def first(block, depth):
         depth = list(depth)
@@ -187,8 +200,8 @@
         ud_send[e] = depth[e]
     for away in range(1, n_beam):
         beam_copy(away).start()
-    pl.semaphore_wait(relay_one, 2)
-    relay(relay_two)
+    hear(0)
+    tell(1)
 
     for away in range(1, n_det):
 
@@ -199,6 +212,16 @@
         @pl.when(det - away < 0)
         def _():
             rc_recv[away] = jnp.zeros_like(rc_send)
+
+    no_halo = jnp.zeros((n_beam, n_e, REACH, ny), F32)
+
+    @pl.when(slab == 0)
+    def _():
+        x_buf[:, :, nz - REACH : nz] = no_halo
+
+    @pl.when(slab == n_slab - 1)
+    def _():
+        x_buf[:, :, 2 * nz : 2 * nz + REACH] = no_halo
 
     deep = lax.broadcasted_iota(jnp.int32, (2 * ny, ny), 0) % ny
     wide = lax.broadcasted_iota(jnp.int32, (2 * ny, ny), 1)
@@ -232,6 +255,8 @@
     for e in range(n_e):
         wm[e] = jnp.dot(own, meas[e], precision=HIGHEST, preferred_element_type=F32)
 
+    hear(1)
+    tell(2)
     for away in range(1, n_beam):
         beam_copy(away).wait_recv()
     upstream = jnp.zeros((n_e, nz, ny), F32)
@@ -259,9 +284,16 @@
     sums = lax.fori_loop(0, blocks, third, (jnp.zeros((nz, ny), F32),) * n_e)
     for e in range(n_e):
         x_buf[0, e, nz : 2 * nz] = sums[e] * up_buf[e]
-    pl.semaphore_wait(relay_two, 2)
+    hear(2)
+    tell(3)
+    send_if = {0: slab < n_slab - 1, 1: slab >= 0, 2: slab > 0}
+    take_if = {0: slab > 0, 1: slab >= 0, 2: slab < n_slab - 1}
     for part, away in lines:
-        line_copy(part, away).start()
+
+        @pl.when(send_if[part])
+        def _():
+            line_copy(part, away).start()
+
 
     def fourth(count, after):
         block = blocks - 1 - count
@@ -278,8 +310,14 @@
 
     lax.fori_loop(0, blocks, fourth, (jnp.zeros((nz, ny), F32),) * n_e)
 
+    hear(3)
+    tell(4)
     for part, away in lines:
-        line_copy(part, away).wait_recv()
+
+        @pl.when(take_if[part])
+        def _():
+            line_copy(part, away).wait_recv()
+
     middle = slice(nz - REACH, 2 * nz + REACH)
     extent = x_buf[0, :, middle]
     for slot in range(1, n_beam):
@@ -308,8 +346,6 @@
         def _():
             column_copy(away).start()
 
-    for away in range(1, n_slab):
-        slab_copy(away, False).start()
     la[:, pl.ds(pl.multiple_of(slab * nz, nz), nz), :] = xl[:, nz : 2 * nz, :]
     shade = [back[e] * further[e] for e in range(n_e)]
     mix, less = [], []
@@ -338,6 +374,17 @@
 
     lax.fori_loop(0, blocks, sixth, 0)
 
+    def take_columns():
+        for away in range(1, n_det):
+
+            @pl.when(det - away >= 0)
+            def _():
+                remote(rc_send, rc_recv.at[away], rc_ss.at[away], rc_rs.at[away], {"det": lax.rem(det + away, n_det)}).wait_recv()
+
+    hear(4)
+    for away in range(1, n_slab):
+        slab_copy(away, False).start()
+    take_columns()
     for away in range(1, n_slab):
         slab_copy(away, True).wait_recv()
     share = n_k // (n_beam * n_slab)
@@ -346,12 +393,6 @@
         signal = jnp.dot(wk[mine, 0 : n_slab * nz], la[e], precision=HIGHEST, preferred_element_type=F32)
         resid[e] = signal * (1.0 / 1.5) - meas[e, mine]
 
-    for away in range(1, n_det):
-
-        @pl.when(det - away >= 0)
-        def _():
-            remote(rc_send, rc_recv.at[away], rc_ss.at[away], rc_rs.at[away], {"det": lax.rem(det + away, n_det)}).wait_recv()
-
     nearer = rc_recv[1]
     for away in range(2, n_det):
         nearer = nearer + rc_recv[away]
@@ -372,7 +413,11 @@
     for away in range(1, n_beam):
         beam_copy(away).wait_send()
     for part, away in lines:
-        line_copy(part, away).wait_send()
+
+        @pl.when(send_if[part])
+        def _():
+            line_copy(part, away).wait_send()
+
     for away in range(1, n_slab):
         slab_copy(away, False).wait_send()
 
@@ -451,8 +496,7 @@
             dma((n_slab,)),
             dma((n_det,)),
             dma((n_det,)),
-            pltpu.SemaphoreType.REGULAR,
-            pltpu.SemaphoreType.REGULAR,
+            pltpu.SemaphoreType.REGULAR((5,)),
         ]
         hbm = pl.BlockSpec(memory_space=pltpu.HBM)
         vmem = pl.BlockSpec(memory_space=pltpu.VMEM)

time: 30.3 us -> 32.2 us (1.063)
  Pallas kernels: 29.6 us -> 31.5 us
    pallas_call x1, Pallas kernels: 26.4 us -> 28.4 us  [shards(): pl.pallas_call(functools.partial(kernel, sizes), out_shape=(pltpu.VMEM((n...]
where the time goes in v5:
time: 32.2 us; the launch traced here: 32.1 us
  Pallas kernels  31.5 us (98%)
  between operations  0.64 us (2%)
    pallas_call x1, Pallas kernels, shards(): pl.pallas_call(functools.partial(kernel, sizes), out_shape=(pltpu.VMEM((n...  28.4 us
    pallas_call x1, Pallas kernels, shards(): pl.pallas_call(finish, out_shape=(jax.ShapeDtypeStruct(concentration.shap...  3.14 us

profile of v5, /device:TPU:1, one launch (start us, length us, event | category | flops | bytes accessed | tf_op | source)
XLA Modules:
  0.0 32.1 jit_solution(3945088102389176221)
XLA Ops:
  0.6 28.4 %shard_map.86 = (f32[4,256,8,128]{3,2,1,0:T(8,128)S(1)}, f32[16,128]{1,0:T(8,128)S(1)}, f32[4,8,128]{2,1,0:T(8,128)S(1)}, f32[4,16,128]{2,1,0:T(8,128)S(1)}) custom-call(f32[4,8,256,128]{3,2,1,0:T(8,128)} %conc.1, f32[4,16]{1,0:T(4,128)} %cross_in.1, f32[4]{0:T(128)} %lam_in.1, s32[4]{0:T(128)} %index_in.1, s32[1,256]{1,0:T(1,128)} %bitcast.3, ...), custom_call_target="tpu_custom_call" | custom-call | tf_op jit(solution)/shard_map/pallas_call | solution.py:504
  29.0 3.1 %shard_map.87 = (f32[4,8,256,128]{3,2,1,0:T(8,128)}, f32[4,16,128]{2,1,0:T(8,128)}) custom-call(f32[4,256,8,128]{3,2,1,0:T(8,128)S(1)} %get-tuple-element.6.part, f32[16,128]{1,0:T(8,128)S(1)} %get-tuple-element.7.near, f32[4,8,128]{2,1,0:T(8,128)S(1)} %get-tuple-element.8.lam_before, f32[4,16,128]{2,1,0:T(8,128)S(1)} %get-tuple-element.9.resid_in), custom_call_target="tpu_custom_call" | custom-call | tf_op jit(solution)/shard_map/pallas_call | solution.py:532

commit v6 on v5

--- a/solution.py
+++ b/solution.py
@@ -284,8 +284,6 @@
     sums = lax.fori_loop(0, blocks, third, (jnp.zeros((nz, ny), F32),) * n_e)
     for e in range(n_e):
         x_buf[0, e, nz : 2 * nz] = sums[e] * up_buf[e]
-    hear(2)
-    tell(3)
     send_if = {0: slab < n_slab - 1, 1: slab >= 0, 2: slab > 0}
     take_if = {0: slab > 0, 1: slab >= 0, 2: slab < n_slab - 1}
     for part, away in lines:
@@ -294,6 +292,8 @@
         def _():
             line_copy(part, away).start()
 
+    hear(2)
+    tell(3)
 
     def fourth(count, after):
         block = blocks - 1 - count
@@ -346,6 +346,9 @@
         def _():
             column_copy(away).start()
 
+    hear(4)
+    for away in range(1, n_slab):
+        slab_copy(away, False).start()
     la[:, pl.ds(pl.multiple_of(slab * nz, nz), nz), :] = xl[:, nz : 2 * nz, :]
     shade = [back[e] * further[e] for e in range(n_e)]
     mix, less = [], []
@@ -381,9 +384,6 @@
             def _():
                 remote(rc_send, rc_recv.at[away], rc_ss.at[away], rc_rs.at[away], {"det": lax.rem(det + away, n_det)}).wait_recv()
 
-    hear(4)
-    for away in range(1, n_slab):
-        slab_copy(away, False).start()
     take_columns()
     for away in range(1, n_slab):
         slab_copy(away, True).wait_recv()

time: 32.2 us -> 30.3 us (0.941)
  Pallas kernels: 31.5 us -> 29.5 us
    pallas_call x1, Pallas kernels: 28.4 us -> 26.4 us  [shards(): pl.pallas_call(functools.partial(kernel, sizes), out_shape=(pltpu.VMEM((n...]
where the time goes in v6:
time: 30.3 us; the launch traced here: 30.2 us
  Pallas kernels  29.5 us (97%)
  between operations  0.64 us (2%)
    pallas_call x1, Pallas kernels, shards(): pl.pallas_call(functools.partial(kernel, sizes), out_shape=(pltpu.VMEM((n...  26.4 us
    pallas_call x1, Pallas kernels, shards(): pl.pallas_call(finish, out_shape=(jax.ShapeDtypeStruct(concentration.shap...  3.14 us

profile of v6, /device:TPU:1, one launch (start us, length us, event | category | flops | bytes accessed | tf_op | source)
XLA Modules:
  0.0 30.2 jit_solution(15474246978942508807)
XLA Ops:
  0.6 26.4 %shard_map.86 = (f32[4,256,8,128]{3,2,1,0:T(8,128)S(1)}, f32[16,128]{1,0:T(8,128)S(1)}, f32[4,8,128]{2,1,0:T(8,128)S(1)}, f32[4,16,128]{2,1,0:T(8,128)S(1)}) custom-call(f32[4,8,256,128]{3,2,1,0:T(8,128)} %conc.1, f32[4,16]{1,0:T(4,128)} %cross_in.1, f32[4]{0:T(128)} %lam_in.1, s32[4]{0:T(128)} %index_in.1, s32[1,256]{1,0:T(1,128)} %bitcast.3, ...), custom_call_target="tpu_custom_call" | custom-call | tf_op jit(solution)/shard_map/pallas_call | solution.py:504
  27.0 3.1 %shard_map.87 = (f32[4,8,256,128]{3,2,1,0:T(8,128)}, f32[4,16,128]{2,1,0:T(8,128)}) custom-call(f32[4,256,8,128]{3,2,1,0:T(8,128)S(1)} %get-tuple-element.6.part, f32[16,128]{1,0:T(8,128)S(1)} %get-tuple-element.7.near, f32[4,8,128]{2,1,0:T(8,128)S(1)} %get-tuple-element.8.lam_before, f32[4,16,128]{2,1,0:T(8,128)S(1)} %get-tuple-element.9.resid_in), custom_call_target="tpu_custom_call" | custom-call | tf_op jit(solution)/shard_map/pallas_call | solution.py:532

commit v7 on v6

--- a/solution.py
+++ b/solution.py
@@ -257,6 +257,8 @@
 
     hear(1)
     tell(2)
+    hear(2)
+    tell(3)
     for away in range(1, n_beam):
         beam_copy(away).wait_recv()
     upstream = jnp.zeros((n_e, nz, ny), F32)
@@ -292,8 +294,8 @@
         def _():
             line_copy(part, away).start()
 
-    hear(2)
-    tell(3)
+    hear(3)
+    tell(4)
 
     def fourth(count, after):
         block = blocks - 1 - count
@@ -310,19 +312,30 @@
 
     lax.fori_loop(0, blocks, fourth, (jnp.zeros((nz, ny), F32),) * n_e)
 
-    hear(3)
-    tell(4)
-    for part, away in lines:
-
-        @pl.when(take_if[part])
-        def _():
-            line_copy(part, away).wait_recv()
-
-    middle = slice(nz - REACH, 2 * nz + REACH)
-    extent = x_buf[0, :, middle]
-    for slot in range(1, n_beam):
-        extent = extent + x_buf[slot, :, middle]
-    xl[:, middle] = extent
+    def take_lines(wanted):
+        for part, away in lines:
+            if part in wanted:
+
+                @pl.when(take_if[part])
+                def _():
+                    line_copy(part, away).wait_recv()
+
+    def gather_lines(rows):
+        total = x_buf[0, :, rows]
+        for slot in range(1, n_beam):
+            total = total + x_buf[slot, :, rows]
+        xl[:, rows] = total
+        return total
+
+    take_lines((1,))
+    own_lines = gather_lines(slice(nz, 2 * nz))
+    hear(4)
+    for away in range(1, n_slab):
+        slab_copy(away, False).start()
+    la[:, pl.ds(pl.multiple_of(slab * nz, nz), nz), :] = own_lines
+    take_lines((0, 2))
+    gather_lines(slice(nz - REACH, nz))
+    gather_lines(slice(2 * nz, 2 * nz + REACH))
     further = jnp.zeros((n_e, nz, ny), F32)
     for slot in range(1, n_beam):
         further = further + jnp.where(beam + slot < n_beam, 1.0, 0.0) * x_buf[slot, :, nz : 2 * nz]
@@ -346,10 +359,6 @@
         def _():
             column_copy(away).start()
 
-    hear(4)
-    for away in range(1, n_slab):
-        slab_copy(away, False).start()
-    la[:, pl.ds(pl.multiple_of(slab * nz, nz), nz), :] = xl[:, nz : 2 * nz, :]
     shade = [back[e] * further[e] for e in range(n_e)]
     mix, less = [], []
     for s in range(n_s):

time: 30.3 us -> 29.6 us (0.977)
  Pallas kernels: 29.5 us -> 28.8 us
    pallas_call x1, Pallas kernels: 26.4 us -> 25.7 us  [shards(): pl.pallas_call(functools.partial(kernel, sizes), out_shape=(pltpu.VMEM((n...]
where the time goes in v7:
time: 29.6 us; the launch traced here: 29.5 us
  Pallas kernels  28.8 us (97%)
  between operations  0.64 us (2%)
    pallas_call x1, Pallas kernels, shards(): pl.pallas_call(functools.partial(kernel, sizes), out_shape=(pltpu.VMEM((n...  25.7 us
    pallas_call x1, Pallas kernels, shards(): pl.pallas_call(finish, out_shape=(jax.ShapeDtypeStruct(concentration.shap...  3.14 us

profile of v7, /device:TPU:1, one launch (start us, length us, event | category | flops | bytes accessed | tf_op | source)
XLA Modules:
  0.0 29.5 jit_solution(4716735160225591197)
XLA Ops:
  0.6 25.7 %shard_map.86 = (f32[4,256,8,128]{3,2,1,0:T(8,128)S(1)}, f32[16,128]{1,0:T(8,128)S(1)}, f32[4,8,128]{2,1,0:T(8,128)S(1)}, f32[4,16,128]{2,1,0:T(8,128)S(1)}) custom-call(f32[4,8,256,128]{3,2,1,0:T(8,128)} %conc.1, f32[4,16]{1,0:T(4,128)} %cross_in.1, f32[4]{0:T(128)} %lam_in.1, s32[4]{0:T(128)} %index_in.1, s32[1,256]{1,0:T(1,128)} %bitcast.3, ...), custom_call_target="tpu_custom_call" | custom-call | tf_op jit(solution)/shard_map/pallas_call | solution.py:513
  26.3 3.1 %shard_map.87 = (f32[4,8,256,128]{3,2,1,0:T(8,128)}, f32[4,16,128]{2,1,0:T(8,128)}) custom-call(f32[4,256,8,128]{3,2,1,0:T(8,128)S(1)} %get-tuple-element.6.part, f32[16,128]{1,0:T(8,128)S(1)} %get-tuple-element.7.near, f32[4,8,128]{2,1,0:T(8,128)S(1)} %get-tuple-element.8.lam_before, f32[4,16,128]{2,1,0:T(8,128)S(1)} %get-tuple-element.9.resid_in), custom_call_target="tpu_custom_call" | custom-call | tf_op jit(solution)/shard_map/pallas_call | solution.py:541

commit v8 on v7

--- a/solution.py
+++ b/solution.py
@@ -37,7 +37,7 @@
 
 
 def kernel(
-    sizes, conc, cross_in, lam_in, index_in, offset_in, weight_in, measured, part_out, near_out, lam_out, resid,
+    sizes, conc, cross_in, lam_in, index_in, offset_in, weight_in, measured, part_out, near_out, lam_out, la_out, wk_out, meas_out,
     cross, lam, index, offset, weight, c_buf, em, inc, dmp, hl, meas, wt, wx, wk, band, wm, up_buf,
     ra_send, ra_recv, ud_send, ud_recv, x_buf, xl, la, rc_send, rc_recv,
     in_sem, small_sem, meas_sem, ra_ss, ra_rs, ud_ss, ud_rs, x_ss, x_rs, la_ss, la_rs, rc_ss, rc_rs, relays,
@@ -393,48 +393,48 @@
             def _():
                 remote(rc_send, rc_recv.at[away], rc_ss.at[away], rc_rs.at[away], {"det": lax.rem(det + away, n_det)}).wait_recv()
 
+    share = n_k // (n_beam * n_slab)
+    mine = pl.ds(pl.multiple_of((beam * n_slab + slab) * share, share), share)
+    wk_out[...] = wk[mine]
+    meas_out[...] = meas[:, mine]
+    for s in range(n_s):
+        lam_out[s] = jnp.full((nz, ny), lam_before[s], F32)
+    for away in range(1, n_det):
+
+        @pl.when(det - away >= 0)
+        def _():
+            depth_copy(away).wait_send()
+
+    for away in range(1, n_beam):
+        beam_copy(away).wait_send()
+    for part, away in lines:
+
+        @pl.when(send_if[part])
+        def _():
+            line_copy(part, away).wait_send()
+
     take_columns()
     for away in range(1, n_slab):
         slab_copy(away, True).wait_recv()
-    share = n_k // (n_beam * n_slab)
-    mine = pl.ds(pl.multiple_of((beam * n_slab + slab) * share, share), share)
-    for e in range(n_e):
-        signal = jnp.dot(wk[mine, 0 : n_slab * nz], la[e], precision=HIGHEST, preferred_element_type=F32)
-        resid[e] = signal * (1.0 / 1.5) - meas[e, mine]
-
+    la_out[...] = la[...]
     nearer = rc_recv[1]
     for away in range(2, n_det):
         nearer = nearer + rc_recv[away]
     near_out[...] = nearer
-    for s in range(n_s):
-        lam_out[s] = jnp.full((nz, ny), lam_before[s], F32)
-
-    for away in range(1, n_det):
-
-        @pl.when(det - away >= 0)
-        def _():
-            depth_copy(away).wait_send()
+
+    for away in range(1, n_det):
 
         @pl.when(det + away < n_det)
         def _():
             column_copy(away).wait_send()
-
-    for away in range(1, n_beam):
-        beam_copy(away).wait_send()
-    for part, away in lines:
-
-        @pl.when(send_if[part])
-        def _():
-            line_copy(part, away).wait_send()
 
     for away in range(1, n_slab):
         slab_copy(away, False).wait_send()
 
 
-def finish(part, near, lam_before, resid_in, out, resid, buf, out_sem):
+def finish(part, near, lam_before, la, wk, meas, out, resid, buf, out_sem):
     n_s, nx, nz, ny = part.shape
     step = nx // STORES
-    resid[...] = resid_in[...]
     pieces = spread(near[...])
 
     def store(chunk, z):
@@ -449,6 +449,9 @@
                 buf[s, rows] = part[s, rows] - lam_before[s] * shift
         for z in range(nz):
             store(chunk, z).start()
+    for e in range(la.shape[0]):
+        signal = jnp.dot(wk[:, 0 : la.shape[1]], la[e], precision=HIGHEST, preferred_element_type=F32)
+        resid[e] = signal * (1.0 / 1.5) - meas[e]
     for chunk in range(STORES):
         for z in range(nz):
             store(chunk, z).wait()
@@ -516,10 +519,12 @@
                 pltpu.VMEM((n_s, nx, nz, ny), F32),
                 pltpu.VMEM(compact, F32),
                 pltpu.VMEM((n_s, nz, ny), F32),
+                pltpu.VMEM((n_e, n_slab * nz, ny), F32),
+                pltpu.VMEM((share, 128), F32),
                 pltpu.VMEM(share_shape, F32),
             ),
             in_specs=[hbm] * 7,
-            out_specs=(vmem,) * 4,
+            out_specs=(vmem,) * 6,
             scratch_shapes=scratch,
             compiler_params=pltpu.CompilerParams(
                 collective_id=0, has_side_effects=True, vmem_limit_bytes=28 * 2**20
@@ -544,7 +549,7 @@
                 jax.ShapeDtypeStruct(concentration.shape, F32),
                 jax.ShapeDtypeStruct(share_shape, F32),
             ),
-            in_specs=[vmem] * 4,
+            in_specs=[vmem] * 6,
             out_specs=(hbm, vmem),
             scratch_shapes=[pltpu.VMEM((n_s, nx, nz, ny), F32), dma((STORES, nz))],
             compiler_params=pltpu.CompilerParams(vmem_limit_bytes=16 * 2**20),

time: 29.6 us -> 29.4 us (level)
  no operation moved by 1% of the time
where the time goes in v8:
time: 29.4 us; the launch traced here: 29.3 us
  Pallas kernels  28.6 us (97%)
  between operations  0.64 us (2%)
    pallas_call x1, Pallas kernels, shards(): pl.pallas_call(functools.partial(kernel, sizes), out_shape=(pltpu.VMEM((n...  25.5 us
    pallas_call x1, Pallas kernels, shards(): pl.pallas_call(finish, out_shape=(jax.ShapeDtypeStruct(concentration.shap...  3.14 us

profile of v8, /device:TPU:1, one launch (start us, length us, event | category | flops | bytes accessed | tf_op | source)
XLA Modules:
  0.0 29.3 jit_solution(14533630710357484291)
XLA Ops:
  0.6 25.5 %shard_map.86 = (f32[4,256,8,128]{3,2,1,0:T(8,128)S(1)}, f32[16,128]{1,0:T(8,128)S(1)}, f32[4,8,128]{2,1,0:T(8,128)S(1)}, f32[4,32,128]{2,1,0:T(8,128)S(1)}, f32...) custom-call(f32[4,8,256,128]{3,2,1,0:T(8,128)} %conc.1, f32[4,16]{1,0:T(4,128)} %cross_in.1, f32[4]{0:T(128)} %lam_in.1, ...), custom_call_target="tpu_custom_call" | custom-call | tf_op jit(solution)/shard_map/pallas_call | solution.py:516
  26.1 3.1 %shard_map.87 = (f32[4,8,256,128]{3,2,1,0:T(8,128)}, f32[4,16,128]{2,1,0:T(8,128)}) custom-call(f32[4,256,8,128]{3,2,1,0:T(8,128)S(1)} %get-tuple-element.8.part, f32[16,128]{1,0:T(8,128)S(1)} %get-tuple-element.9.near, f32[4,8,128]{2,1,0:T(8,128)S(1)} %get-tuple-element.10.lam_before, f32[4,32,128]{2,1,0:T(8,128)S(1)} %get-tuple-element.11.la, ...), custom_call_target="tpu_custom_call" | custom-call | tf_op jit(solution)/shard_map/pallas_call | solution.py:546

commit v9 on v8

--- a/solution.py
+++ b/solution.py
@@ -139,7 +139,8 @@
         )
 
     order = sorted(range(n_beam), key=lambda away: abs(2 * away - n_beam))
-    lines = [(part, away) for away in order for part in (0, 2)] + [(1, away) for away in order if away]
+    halos = [(part, away) for away in order for part in (0, 2)]
+    lines = halos[:2] + [(1, away) for away in order if away] + halos[2:]
 
     def slab_copy(away, receiving):
         source = slab_at(away) if receiving else slab

time: 29.4 us -> 29 us (0.986)
  Pallas kernels: 28.6 us -> 28.3 us
    pallas_call x1, Pallas kernels: 25.5 us -> 25.1 us  [shards(): pl.pallas_call(functools.partial(kernel, sizes), out_shape=(pltpu.VMEM((n...]
where the time goes in v9:
time: 29 us; the launch traced here: 28.9 us
  Pallas kernels  28.3 us (98%)
  between operations  0.64 us (2%)
    pallas_call x1, Pallas kernels, shards(): pl.pallas_call(functools.partial(kernel, sizes), out_shape=(pltpu.VMEM((n...  25.1 us
    pallas_call x1, Pallas kernels, shards(): pl.pallas_call(finish, out_shape=(jax.ShapeDtypeStruct(concentration.shap...  3.14 us

profile of v9, /device:TPU:1, one launch (start us, length us, event | category | flops | bytes accessed | tf_op | source)
XLA Modules:
  0.0 28.9 jit_solution(9633581680258526625)
XLA Ops:
  0.6 25.1 %shard_map.86 = (f32[4,256,8,128]{3,2,1,0:T(8,128)S(1)}, f32[16,128]{1,0:T(8,128)S(1)}, f32[4,8,128]{2,1,0:T(8,128)S(1)}, f32[4,32,128]{2,1,0:T(8,128)S(1)}, f32...) custom-call(f32[4,8,256,128]{3,2,1,0:T(8,128)} %conc.1, f32[4,16]{1,0:T(4,128)} %cross_in.1, f32[4]{0:T(128)} %lam_in.1, ...), custom_call_target="tpu_custom_call" | custom-call | tf_op jit(solution)/shard_map/pallas_call | solution.py:517
  25.8 3.1 %shard_map.87 = (f32[4,8,256,128]{3,2,1,0:T(8,128)}, f32[4,16,128]{2,1,0:T(8,128)}) custom-call(f32[4,256,8,128]{3,2,1,0:T(8,128)S(1)} %get-tuple-element.8.part, f32[16,128]{1,0:T(8,128)S(1)} %get-tuple-element.9.near, f32[4,8,128]{2,1,0:T(8,128)S(1)} %get-tuple-element.10.lam_before, f32[4,32,128]{2,1,0:T(8,128)S(1)} %get-tuple-element.11.la, ...), custom_call_target="tpu_custom_call" | custom-call | tf_op jit(solution)/shard_map/pallas_call | solution.py:547
